TPU v7x, 512 devices: a whole 4x8x8 slice. The times are simulated.
512 devices in a mesh: pipe: 8 (over y_lo, x), expert: 16 (over z, core), dp: 4 (over y_hi).
Axes of the slice: x: 4, y: 8 (y_hi: 4, y_lo: 2; y = y_hi * 2 + y_lo), z: 8, core: 2. Of those that a mesh axis runs over, the one named last changes fastest.
Arguments:
- in_flight: bfloat16 [8, 4096, 2048], P('pipe', ('expert', 'dp')), may hold values from -6 to 6
- fresh_grads: bfloat16 [1, 4096, 2048], P(None, ('expert', 'dp')), may hold values from -6 to 6
- saved_inputs: bfloat16 [2, 8, 4096, 2048], P(None, 'pipe', ('expert', 'dp')), may hold values from -6 to 6
- norm_gain: bfloat16 [8, 2048], P('pipe'), may hold values from 0.099609375 to 1.8984375
- expert_ids: int32 [2, 8, 4096, 2], P(None, 'pipe', ('expert', 'dp')), may hold values from 0 to 7, all different within a row; in each aligned block of 64 rows (0 to 63, 64 to 127, ..., all dimensions but the last counted through in order) at most 24 rows name the same one
- gate_weights: float32 [2, 8, 4096, 2], P(None, 'pipe', ('expert', 'dp')), may hold values from 0.1 to 1
- up_weights: bfloat16 [8, 5632, 2048], P('pipe', 'expert'), may hold values from -0.125 to 0.125
- down_weights: bfloat16 [8, 5632, 2048], P('pipe', 'expert'), may hold values from -0.21875 to 0.21875
Outputs:
- input_grads: bfloat16 [2, 8, 4096, 2048], P(None, 'pipe', ('expert', 'dp'))
- up_grads: bfloat16 [8, 5632, 2048], P('pipe', 'expert', 'dp')
- down_grads: bfloat16 [8, 5632, 2048], P('pipe', 'expert', 'dp')
Inputs may be any that keep to these rules, and one draw needn't show every extreme that they name: `expert_ids`: each row names two different experts. Among the 64 frames of one device's aligned block of one step and section, no expert is named more than 24 times, a bound that some block reaches.
All inputs are finite; a program needn't handle non-finite values.
Results may differ from a plain program's by a relative error of at most 0.015.
Values may be sent and summed in bfloat16 or wider, within the bound.
A program may use at most 64 MiB of HBM per device.

v0:
```python
import jax
import jax.numpy as jnp
from jax import lax
from jax.sharding import PartitionSpec as P

norm_eps = 1e-06


def passed_along(shard, axis, by):
    count = lax.axis_size(axis)
    pairs = [(i, i + by) for i in range(count) if 0 <= i + by < count]
    return lax.ppermute(shard, axis, pairs)


def contract_rows(left, right):
    return lax.dot_general(
        left, right, (((0,), (0,)), ((), ())), preferred_element_type=jnp.float32
    )


def contract_cols(left, right):
    return lax.dot_general(
        left, right, (((1,), (1,)), ((), ())), preferred_element_type=jnp.float32
    )


def expert_work(slot_inputs, slot_grads, up_local, down_local):
    pre_act = contract_cols(slot_inputs, up_local)
    sigma = jax.nn.sigmoid(pre_act)
    activated = (pre_act * sigma).astype(jnp.bfloat16)
    hidden_grad = contract_cols(slot_grads, down_local)
    hidden_grad = (hidden_grad * (sigma * (1.0 + pre_act * (1.0 - sigma)))).astype(jnp.bfloat16)
    partial_grad = jnp.dot(hidden_grad, up_local, preferred_element_type=jnp.float32)
    return (activated, hidden_grad, partial_grad)


def local(
    in_flight,
    fresh_grads,
    saved_inputs,
    norm_gain,
    expert_ids,
    gate_weights,
    up_weights,
    down_weights,
):
    groups = lax.axis_size("expert")
    sections = lax.axis_size("pipe")
    section_index = lax.axis_index("pipe")
    experts = groups // 2
    window = saved_inputs.shape[0]
    frames = saved_inputs.shape[2]
    width = saved_inputs.shape[3]
    capacity = min(frames, 3 * frames // experts)
    pairs = 2 * frames
    slot_count = groups * capacity
    up_local = up_weights[0]
    down_local = down_weights[0]
    gain = norm_gain[0].astype(jnp.float32)
    up_total = jnp.zeros(up_local.shape, jnp.float32)
    down_total = jnp.zeros(down_local.shape, jnp.float32)
    results = []
    incoming = in_flight[0]
    for step_index in range(window):
        if step_index > 0:
            arrived = passed_along(results[-1], "pipe", -1)
            incoming = jnp.where(
                section_index == sections - 1, fresh_grads[step_index - 1], arrived
            )
        inputs = saved_inputs[step_index, 0].astype(jnp.float32)
        scale = lax.rsqrt(jnp.mean(inputs * inputs, axis=-1, keepdims=True) + norm_eps)
        normed = (inputs * scale * gain).astype(jnp.bfloat16)
        chosen_ids = expert_ids[step_index, 0].reshape(pairs)
        gates = gate_weights[step_index, 0]
        scaled = (
            (gates[:, :, None] * incoming.astype(jnp.float32)[:, None, :])
            .astype(jnp.bfloat16)
            .reshape(pairs, width)
        )
        normed_pairs = jnp.repeat(normed, 2, axis=0)
        member = (chosen_ids[:, None] == jnp.arange(experts, dtype=jnp.int32)[None, :]).astype(
            jnp.int32
        )
        earlier = jnp.cumsum(member, axis=0) - member
        slot_of = jnp.sum(earlier * member, axis=1)
        targets = 2 * chosen_ids * capacity + slot_of
        places = jnp.arange(slot_count, dtype=jnp.int32)[:, None]
        select = ((places == targets[None, :]) | (places == targets[None, :] + capacity)).astype(
            jnp.bfloat16
        )
        send_inputs = (
            jnp.dot(select, normed_pairs, preferred_element_type=jnp.float32)
            .astype(jnp.bfloat16)
            .reshape(groups, capacity, width)
        )
        send_grads = (
            jnp.dot(select, scaled, preferred_element_type=jnp.float32)
            .astype(jnp.bfloat16)
            .reshape(groups, capacity, width)
        )
        got_inputs, got_grads = (
            lax.all_to_all(send_inputs, "expert", split_axis=0, concat_axis=0, tiled=True),
            lax.all_to_all(send_grads, "expert", split_axis=0, concat_axis=0, tiled=True),
        )
        slot_inputs = got_inputs.reshape(slot_count, width)
        slot_grads = got_grads.reshape(slot_count, width)
        activated, hidden_grad, partial_grad = expert_work(
            slot_inputs, slot_grads, up_local, down_local
        )
        returned = lax.all_to_all(
            partial_grad.astype(jnp.bfloat16).reshape(groups, capacity, width),
            "expert",
            split_axis=0,
            concat_axis=0,
            tiled=True,
        )
        feature_pairs = contract_rows(select, returned.reshape(slot_count, width))
        feature_grad = feature_pairs.reshape(frames, 2, width).sum(axis=1)
        weighted = gain * feature_grad
        result = incoming.astype(jnp.float32) + scale * weighted
        result = result - inputs * (scale * scale * scale) * jnp.mean(
            inputs * weighted, axis=-1, keepdims=True
        )
        results.append(result.astype(jnp.bfloat16))
        up_total = up_total + contract_rows(hidden_grad, slot_inputs)
        down_total = down_total + contract_rows(activated, slot_grads)
    up_sum, down_sum = (
        lax.psum_scatter(
            up_total.astype(jnp.bfloat16), "dp", scatter_dimension=1, tiled=True
        ).astype(jnp.float32),
        lax.psum_scatter(
            down_total.astype(jnp.bfloat16), "dp", scatter_dimension=1, tiled=True
        ).astype(jnp.float32),
    )
    input_grads = jnp.stack(results, 0)[:, None]
    return (input_grads, up_sum.astype(jnp.bfloat16)[None], down_sum.astype(jnp.bfloat16)[None])


def solution(mesh):
    in_specs = (
        P("pipe", ("expert", "dp"), None),
        P(None, ("expert", "dp"), None),
        P(None, "pipe", ("expert", "dp"), None),
        P("pipe", None),
        P(None, "pipe", ("expert", "dp"), None),
        P(None, "pipe", ("expert", "dp"), None),
        P("pipe", "expert", None),
        P("pipe", "expert", None),
    )
    out_specs = (
        P(None, "pipe", ("expert", "dp"), None),
        P("pipe", "expert", "dp"),
        P("pipe", "expert", "dp"),
    )
    return jax.shard_map(local, mesh=mesh, in_specs=in_specs, out_specs=out_specs, check_vma=False)
```

profile of v0, /device:TPU:1, one launch (start us, length us, event | category | flops | bytes accessed | tf_op | source)
XLA Modules:
  0.0 347.1 jit_solution(285864885908206363)
XLA Ops:
  7.2 1.3 fusion.76
  9.2 0.7 mul.328
  9.9 1.1 fusion.30
  11.0 0.5 multiply_multiply_fusion.1
  11.5 0.5 copy-done.18
  12.0 1.1 fusion.32
  13.1 0.3 broadcast_in_dim.10
  13.6 1.7 convolution_convert_fusion.4
  15.4 12.0 %all-to-all-start.1 = ((bf16[16,24,2048]{2,1,0:T(8,128)(2,1)}), bf16[16,24,2048]{2,1,0:T(8,128)(2,1)S(1)}, u32[]{:S(2)}, u32[]{:S(2)}) async-start(bf16[16,24,2048]{2,1,0:T(8,128)(2,1)} %bitcast.127), calls=%async_computation.1 | async-start | bytes 3145728 | tf_op jit(solution)/shard_map/all_to_all | solution.py:102
  27.3 0.6 fusion.77
  28.2 1.5 mul.278
  29.8 2.9 mul.279
  32.7 3.0 convolution_convert_fusion.5
  35.7 30.1 %all-to-all-done.1 = bf16[16,24,2048]{2,1,0:T(8,128)(2,1)S(1)} async-done(((bf16[16,24,2048]{2,1,0:T(8,128)(2,1)}), bf16[16,24,2048]{2,1,0:T(8,128)(2,1)S(1)}, u32[]{:S(2)}, u32[]{:S(2)}) %all-to-all-start.1) | async-done | bytes 1572896 | tf_op jit(solution)/shard_map/all_to_all | solution.py:102
  65.8 4.3 %all-to-all-start = ((bf16[16,24,2048]{2,1,0:T(8,128)(2,1)}), bf16[16,24,2048]{2,1,0:T(8,128)(2,1)}, u32[]{:S(2)}, u32[]{:S(2)}) async-start(bf16[16,24,2048]{2,1,0:T(8,128)(2,1)} %bitcast.129), calls=%async_computation | async-start | bytes 3145728 | tf_op jit(solution)/shard_map/all_to_all | solution.py:103
  70.1 1.7 fusion.6
  71.8 36.7 %all-to-all-done = bf16[16,24,2048]{2,1,0:T(8,128)(2,1)} async-done(((bf16[16,24,2048]{2,1,0:T(8,128)(2,1)}), bf16[16,24,2048]{2,1,0:T(8,128)(2,1)}, u32[]{:S(2)}, u32[]{:S(2)}) %all-to-all-start) | async-done | bytes 1572896 | tf_op jit(solution)/shard_map/all_to_all | solution.py:103
  108.6 2.9 fusion.21
  111.5 2.2 convolution_convert_fusion.1
  113.7 4.3 %all-to-all-start.2 = ((bf16[16,24,2048]{2,1,0:T(8,128)(2,1)}), bf16[16,24,2048]{2,1,0:T(8,128)(2,1)S(1)}, u32[]{:S(2)}, u32[]{:S(2)}) async-start(bf16[16,24,2048]{2,1,0:T(8,128)(2,1)} %bitcast.123), calls=%async_computation.2 | async-start | bytes 3145728 | tf_op jit(solution)/shard_map/all_to_all | solution.py:110
  117.9 0.7 fusion.54
  118.7 1.5 or.29
  120.2 1.3 copy.18
  121.5 0.9 reshape_squeeze.7
  122.4 0.7 fusion.72
  123.1 1.6 reduce_window_sum.18
  124.7 1.0 select_reduce_fusion
  125.7 0.6 broadcast_add_fusion
  126.3 30.1 %all-to-all-done.2 = bf16[16,24,2048]{2,1,0:T(8,128)(2,1)S(1)} async-done(((bf16[16,24,2048]{2,1,0:T(8,128)(2,1)}), bf16[16,24,2048]{2,1,0:T(8,128)(2,1)S(1)}, u32[]{:S(2)}, u32[]{:S(2)}) %all-to-all-start.2) | async-done | bytes 1572896 | tf_op jit(solution)/shard_map/all_to_all | solution.py:110
  156.4 1.2 copy-done.2
  157.6 2.0 convolution_reduce_fusion.1
  159.6 0.2 fusion.39
  159.8 0.5 multiply_multiply_fusion
  160.4 1.0 fusion.41
  161.4 0.3 broadcast_in_dim.11
  161.7 1.0 reshape.345
  162.7 2.8 convolution_convert_fusion.2
  165.5 4.4 %all-to-all-start.4 = ((bf16[16,24,2048]{2,1,0:T(8,128)(2,1)}), bf16[16,24,2048]{2,1,0:T(8,128)(2,1)}, u32[]{:S(2)}, u32[]{:S(2)}) async-start(bf16[16,24,2048]{2,1,0:T(8,128)(2,1)} %bitcast.126), calls=%async_computation.4 | async-start | bytes 3145728 | tf_op jit(solution)/shard_map/all_to_all | solution.py:102
  170.0 1.3 collective-permute-start
  171.4 0.7 mul.307
  172.0 7.8 %collective-permute-done = bf16[64,2048]{1,0:T(8,128)(2,1)} collective-permute-done((bf16[64,2048]{1,0:T(8,128)(2,1)S(1)}, bf16[64,2048]{1,0:T(8,128)(2,1)}, u32[]{:S(2)}, u32[]{:S(2)}) %collective-permute-start) | collective-permute-done | bytes 262176 | tf_op jit(solution)/shard_map/ppermute | solution.py:12
  179.8 1.0 fusion.53
  180.8 1.7 mul.309
  182.5 2.9 mul.310
  185.4 3.0 convolution_convert_fusion.3
  188.5 20.0 %all-to-all-done.4 = bf16[16,24,2048]{2,1,0:T(8,128)(2,1)} async-done(((bf16[16,24,2048]{2,1,0:T(8,128)(2,1)}), bf16[16,24,2048]{2,1,0:T(8,128)(2,1)}, u32[]{:S(2)}, u32[]{:S(2)}) %all-to-all-start.4) | async-done | bytes 1572896 | tf_op jit(solution)/shard_map/all_to_all | solution.py:102
  208.4 4.3 %all-to-all-start.3 = ((bf16[16,24,2048]{2,1,0:T(8,128)(2,1)}), bf16[16,24,2048]{2,1,0:T(8,128)(2,1)}, u32[]{:S(2)}, u32[]{:S(2)}) async-start(bf16[16,24,2048]{2,1,0:T(8,128)(2,1)} %bitcast.128), calls=%async_computation.3 | async-start | bytes 3145728 | tf_op jit(solution)/shard_map/all_to_all | solution.py:103
  212.8 0.2 reduce-scatter.5.cloned.1.call-start
  213.0 4.1 %fusion.49 = f32[352,2048]{1,0:T(8,128)} fusion(bf16[384,2048]{1,0:T(8,128)(2,1)} %bitcast.4, f32[384,352]{0,1:T(8,128)} %fusion.6), kind=kOutput, calls=%fused_computation.67 | convolution fusion | flops 554323968 | bytes 4997120 | tf_op jit(solution)/shard_map/dot_general | solution.py:16
  217.1 3.2 fusion.3
  220.2 31.0 %all-to-all-done.3 = bf16[16,24,2048]{2,1,0:T(8,128)(2,1)} async-done(((bf16[16,24,2048]{2,1,0:T(8,128)(2,1)}), bf16[16,24,2048]{2,1,0:T(8,128)(2,1)}, u32[]{:S(2)}, u32[]{:S(2)}) %all-to-all-start.3) | async-done | bytes 1572896 | tf_op jit(solution)/shard_map/all_to_all | solution.py:103
  251.2 4.5 %fusion.1 = bf16[352,2048]{1,0:T(8,128)(2,1)} fusion(f32[352,2048]{1,0:T(8,128)} %fusion.49, bf16[384,2048]{1,0:T(8,128)(2,1)} %bitcast.17, f32[384,352]{0,1:T(8,128)} %fusion.3), kind=kOutput, calls=%fused_computation.9 | convolution fusion | flops 555765760 | bytes 6438912 | tf_op jit(solution)/shard_map/dot_general | solution.py:16
  255.8 2.9 fusion.18
  258.7 2.2 convolution_convert_fusion
  260.9 4.4 %all-to-all-start.5 = ((bf16[16,24,2048]{2,1,0:T(8,128)(2,1)}), bf16[16,24,2048]{2,1,0:T(8,128)(2,1)}, u32[]{:S(2)}, u32[]{:S(2)}) async-start(bf16[16,24,2048]{2,1,0:T(8,128)(2,1)} %bitcast.121), calls=%async_computation.5 | async-start | bytes 3145728 | tf_op jit(solution)/shard_map/all_to_all | solution.py:110
  265.4 2.4 fusion.78
  267.8 3.6 %fusion = bf16[352,2048]{1,0:T(8,128)(2,1)} fusion(f32[352,2048]{1,0:T(8,128)S(1)} %fusion.78, bf16[384,352]{0,1:T(8,128)(2,1)S(1)} %copy-done.9, bf16[384,2048]{1,0:T(8,128)(2,1)} %bitcast.20), kind=kOutput, calls=%fused_computation.8 | convolution fusion | flops 555089920 | bytes 6168576 | tf_op jit(solution)/shard_map/dot_general | solution.py:16
  271.5 0.7 or.32
  272.2 0.9 fusion.29
  273.1 30.7 %all-to-all-done.5 = bf16[16,24,2048]{2,1,0:T(8,128)(2,1)} async-done(((bf16[16,24,2048]{2,1,0:T(8,128)(2,1)}), bf16[16,24,2048]{2,1,0:T(8,128)(2,1)}, u32[]{:S(2)}, u32[]{:S(2)}) %all-to-all-start.5) | async-done | bytes 1572896 | tf_op jit(solution)/shard_map/all_to_all | solution.py:110
  303.8 1.9 convolution_reduce_fusion
  306.0 0.2 fusion.52
  306.2 0.8 maximum_bitcast_fusion
  307.1 33.2 %reduce-scatter.3.cloned.1.call-done = bf16[352,512]{1,0:T(8,128)(2,1)} async-done(((bf16[352,2048]{1,0:T(8,128)(2,1)}), bf16[352,512]{1,0:T(8,128)(2,1)}) %reduce-scatter.3.cloned.1.call-update) | async-done | bytes 360464 | tf_op jit(solution)/shard_map/reduce_scatter | solution.py:128
  (72 shorter events, 1.7 us)
Async XLA Ops:
  7.2 62.9 %copy-start = (bf16[1,352,2048]{2,1,0:T(8,128)(2,1)S(1)}, bf16[1,352,2048]{2,1,0:T(8,128)(2,1)}, u32[]{:S(2)}) copy-start(bf16[1,352,2048]{2,1,0:T(8,128)(2,1)} %param.14) | copy-start | bytes 4325380
  11.5 0.5 copy-start.18
  15.4 12.0 %copy-start.26 = (f32[2,1,64,2]{2,3,1,0:T(2,128)S(1)}, f32[2,1,64,2]{2,3,1,0:T(2,128)}, u32[]{:S(2)}) copy-start(f32[2,1,64,2]{2,3,1,0:T(2,128)} %param.13) | copy-start | bytes 3076
  15.4 12.8 %copy-start.4 = (bf16[1,64,2048]{2,1,0:T(8,128)(2,1)S(1)}, bf16[1,64,2048]{2,1,0:T(8,128)(2,1)}, u32[]{:S(2)}) copy-start(bf16[1,64,2048]{2,1,0:T(8,128)(2,1)} %param.8) | copy-start | bytes 786436
  15.4 50.4 %all-to-all-start.1 = ((bf16[16,24,2048]{2,1,0:T(8,128)(2,1)}), bf16[16,24,2048]{2,1,0:T(8,128)(2,1)S(1)}, u32[]{:S(2)}, u32[]{:S(2)}) async-start(bf16[16,24,2048]{2,1,0:T(8,128)(2,1)} %bitcast.127), calls=%async_computation.1 | async-start | bytes 3145728 | tf_op jit(solution)/shard_map/all_to_all | solution.py:102
  65.8 4.3 %copy-start.3 = (bf16[16,24,2048]{2,1,0:T(8,128)(2,1)}, bf16[16,24,2048]{2,1,0:T(8,128)(2,1)S(1)}, u32[]{:S(2)}) copy-start(bf16[16,24,2048]{2,1,0:T(8,128)(2,1)S(1)} %all-to-all-done.1) | copy-start | bytes 4718596
  65.8 42.8 %all-to-all-start = ((bf16[16,24,2048]{2,1,0:T(8,128)(2,1)}), bf16[16,24,2048]{2,1,0:T(8,128)(2,1)}, u32[]{:S(2)}, u32[]{:S(2)}) async-start(bf16[16,24,2048]{2,1,0:T(8,128)(2,1)} %bitcast.129), calls=%async_computation | async-start | bytes 3145728 | tf_op jit(solution)/shard_map/all_to_all | solution.py:103
  111.5 2.2 copy-start.6
  113.7 42.7 %all-to-all-start.2 = ((bf16[16,24,2048]{2,1,0:T(8,128)(2,1)}), bf16[16,24,2048]{2,1,0:T(8,128)(2,1)S(1)}, u32[]{:S(2)}, u32[]{:S(2)}) async-start(bf16[16,24,2048]{2,1,0:T(8,128)(2,1)} %bitcast.123), calls=%async_computation.2 | async-start | bytes 3145728 | tf_op jit(solution)/shard_map/all_to_all | solution.py:110
  117.9 41.6 %copy-start.1 = (bf16[2,1,64,2048]{3,2,1,0:T(8,128)(2,1)S(1)}, bf16[2,1,64,2048]{3,2,1,0:T(8,128)(2,1)}, u32[]{:S(2)}) copy-start(bf16[2,1,64,2048]{3,2,1,0:T(8,128)(2,1)} %param.10) | copy-start | bytes 1572868
  126.3 59.1 %copy-start.12 = (s32[128]{0:T(128)}, s32[128]{0:T(128)S(1)}, u32[]{:S(2)}) copy-start(s32[128]{0:T(128)S(1)} %get-tuple-element.5) | copy-start | bytes 1540
  156.4 1.2 copy-start.2
  157.6 2.8 copy-start.5
  157.6 2.8 copy-start.19
  157.6 2.8 copy-start.25
  160.3 2.4 copy-start.16
  160.3 2.4 copy-start.21
  160.4 2.4 copy-start.14
  165.5 4.4 %copy-start.11 = (bf16[64,2048]{1,0:T(8,128)(2,1)S(1)}, bf16[64,2048]{1,0:T(8,128)(2,1)}, u32[]{:S(2)}) copy-start(bf16[64,2048]{1,0:T(8,128)(2,1)} %get-tuple-element.10) | copy-start | bytes 786436
  165.5 5.8 %copy-start.23 = (f32[1,1,64,2]{2,3,1,0:T(2,128)S(1)}, f32[1,1,64,2]{2,3,1,0:T(2,128)}, u32[]{:S(2)}) copy-start(f32[1,1,64,2]{2,3,1,0:T(2,128)} %get-tuple-element.13) | copy-start | bytes 1540
  165.5 14.3 %copy-start.10 = (bf16[1,64,2048]{2,1,0:T(8,128)(2,1)S(1)}, bf16[1,64,2048]{2,1,0:T(8,128)(2,1)}, u32[]{:S(2)}) copy-start(bf16[1,64,2048]{2,1,0:T(8,128)(2,1)} %param.9) | copy-start | bytes 786436
  165.5 42.9 %all-to-all-start.4 = ((bf16[16,24,2048]{2,1,0:T(8,128)(2,1)}), bf16[16,24,2048]{2,1,0:T(8,128)(2,1)}, u32[]{:S(2)}, u32[]{:S(2)}) async-start(bf16[16,24,2048]{2,1,0:T(8,128)(2,1)} %bitcast.126), calls=%async_computation.4 | async-start | bytes 3145728 | tf_op jit(solution)/shard_map/all_to_all | solution.py:102
  170.0 9.9 %collective-permute-start = (bf16[64,2048]{1,0:T(8,128)(2,1)S(1)}, bf16[64,2048]{1,0:T(8,128)(2,1)}, u32[]{:S(2)}, u32[]{:S(2)}) collective-permute-start(bf16[64,2048]{1,0:T(8,128)(2,1)S(1)} %copy-done.11), channel_id=1, source_target_pairs={{64,0},{128,64},{192,128},{256,192},{320,256},{384,320},{448,384},... | collective-permute-start | bytes 786440 | tf_op jit(solution)/shard_map/ppermute | solution.py:12
  180.8 4.6 %copy-start.27 = (f32[128]{0:T(128)S(1)}, f32[128]{0:T(128)}, u32[]{:S(2)}) copy-start(f32[128]{0:T(128)} %mul.307) | copy-start | bytes 1540
  208.4 42.8 %all-to-all-start.3 = ((bf16[16,24,2048]{2,1,0:T(8,128)(2,1)}), bf16[16,24,2048]{2,1,0:T(8,128)(2,1)}, u32[]{:S(2)}, u32[]{:S(2)}) async-start(bf16[16,24,2048]{2,1,0:T(8,128)(2,1)} %bitcast.128), calls=%async_computation.3 | async-start | bytes 3145728 | tf_op jit(solution)/shard_map/all_to_all | solution.py:103
  212.8 94.3 %reduce-scatter.5.cloned.1.call-start = ((), (), s32[]{:S(2)}) async-start(), calls=%async_computation.9 | async-start | bytes 1802240 | tf_op jit(solution)/shard_map/reduce_scatter | solution.py:131
  258.7 2.2 copy-start.8
  260.9 4.5 %copy-start.7 = (bf16[384,352]{0,1:T(8,128)(2,1)S(1)}, bf16[384,352]{0,1:T(8,128)(2,1)}, u32[]{:S(2)}) copy-start(bf16[384,352]{0,1:T(8,128)(2,1)} %copy-done.6) | copy-start | bytes 811012
  260.9 42.9 %all-to-all-start.5 = ((bf16[16,24,2048]{2,1,0:T(8,128)(2,1)}), bf16[16,24,2048]{2,1,0:T(8,128)(2,1)}, u32[]{:S(2)}, u32[]{:S(2)}) async-start(bf16[16,24,2048]{2,1,0:T(8,128)(2,1)} %bitcast.121), calls=%async_computation.5 | async-start | bytes 3145728 | tf_op jit(solution)/shard_map/all_to_all | solution.py:110
  265.3 75.0 %reduce-scatter.3.cloned.1.call-start = ((), (), s32[]{:S(2)}) async-start(), calls=%async_computation.8 | async-start | bytes 1802240 | tf_op jit(solution)/shard_map/reduce_scatter | solution.py:128
  265.4 2.4 copy-start.9
  267.8 3.6 %copy-start.13 = (s32[128]{0:T(128)S(1)}, s32[128]{0:T(128)}, u32[]{:S(2)}) copy-start(s32[128]{0:T(128)} %copy-done.12) | copy-start | bytes 1540
  267.8 3.6 %copy-start.15 = (s32[128]{0:T(128)S(1)}, s32[128]{0:T(128)}, u32[]{:S(2)}) copy-start(s32[128]{0:T(128)} %get-tuple-element.6) | copy-start | bytes 1540
  271.4 0.9 copy-start.20
  271.4 0.9 copy-start.22
  273.1 32.9 %copy-start.17 = (f32[64]{0:T(128)S(1)}, f32[64]{0:T(128)}, u32[]{:S(2)}) copy-start(f32[64]{0:T(128)} %copy-done.16) | copy-start | bytes 772
  273.1 32.9 %copy-start.24 = (f32[64]{0:T(128)S(1)}, f32[64]{0:T(128)}, u32[]{:S(2)}) copy-start(f32[64]{0:T(128)} %get-tuple-element.15) | copy-start | bytes 772
Sparse Core Ops, SparseCore 0:
  255.9 39.7 reduce-scatter.4
  299.1 41.1 reduce-scatter.2
where the time goes:
time: 348 us; the launch traced here: 347 us
  waiting for transfers between devices  220 us (63%)
  matrix products  44.1 us (13%)
  starting transfers between devices  35.2 us (10%)
  local copies, waits for them, and re-layouts  20.2 us (6%)
  between operations  14.4 us (4%)
  other arithmetic  13.5 us (4%)
    all_to_all x2, waiting for transfers between devices, local(): lax.all_to_all(send_grads, 'expert', split_axis=0, concat_axis=0, tiled=T...  67.8 us
    all_to_all x2, waiting for transfers between devices, local(): lax.all_to_all(partial_grad.astype(jnp.bfloat16).reshape(groups, capacity...  60.8 us
    all_to_all x2, waiting for transfers between devices, local(): lax.all_to_all(send_inputs, 'expert', split_axis=0, concat_axis=0, tiled=...  50 us
    reduce_scatter x1, waiting for transfers between devices, local(): lax.psum_scatter(up_total.astype(jnp.bfloat16), 'dp', scatter_dimension=1...  33.2 us
    dot_general x6, matrix products, contract_rows(): lax.dot_general(left, right, (((0,), (0,)), ((), ())), preferred_element_...  18.5 us
    all_to_all x2, starting transfers between devices, local(): lax.all_to_all(send_inputs, 'expert', split_axis=0, concat_axis=0, tiled=...  16.4 us
    dot_general x4, matrix products, contract_cols(): lax.dot_general(left, right, (((1,), (1,)), ((), ())), preferred_element_...  10.7 us
    mul x6, local copies, waits for them, and re-layouts, local(): gates[:, :, None] * incoming.astype(jnp.float32)[:, None, :]  9.86 us
  transfers between devices with their start and end apart: 9, of which 8 were waited for; matrix products, arithmetic and copies ran while one was open for 15% of the time, Pallas kernels for 0%

commit v1 on v0

v1 whole, which is shorter than its diff:
```python
import functools

import jax
import jax.numpy as jnp
from jax import lax
from jax.experimental import pallas as pl
from jax.experimental.pallas import tpu as pltpu
from jax.sharding import PartitionSpec as P

norm_eps = 1e-06
MESH = pl.DeviceIdType.MESH
f32 = jnp.float32
bf16 = jnp.bfloat16


def dot(left, right, left_dim, right_dim):
    return lax.dot_general(
        left, right, (((left_dim,), (right_dim,)), ((), ())), preferred_element_type=f32
    )


def kernel(
    chips,
    replicas,
    sections,
    capacity,
    in_flight,
    fresh,
    saved,
    gain,
    ids,
    gates,
    up_hbm,
    down_hbm,
    out_grads,
    out_up,
    out_down,
    up_w,
    down_w,
    select,
    gate_of,
    frames,
    scales,
    snd,
    own,
    sib,
    x_all,
    g_all,
    act_all,
    hid_all,
    slope,
    part_own,
    part_snd,
    part_rcv,
    ret_snd,
    ret_rcv,
    relay_snd,
    relay_rcv,
    rs_snd,
    rs_rcv,
    w_sem,
    disp_s,
    disp_r,
    fwd_s,
    fwd_r,
    part_s,
    part_r,
    ret_s,
    ret_r,
    relay_s,
    relay_r,
    rs_s,
    rs_r,
):
    n, cap = chips, capacity
    block = 2 * cap
    rows, half = frames.shape[2], frames.shape[3]
    tokens = rows // 2
    per_step = n * block
    group = n // 4
    group_rows = 2 * group * cap
    quarter = out_up.shape[2]
    place = lax.axis_index("expert")
    chip, core = place // 2, lax.rem(place, 2)
    section = lax.axis_index("pipe")
    replica = lax.axis_index("dp")

    def chip_at(d):
        return {"expert": 2 * lax.rem(chip + d, n) + core}

    sibling = {"expert": 2 * chip + 1 - core}
    section_before = {"pipe": lax.rem(section + sections - 1, sections)}
    section_after = {"pipe": lax.rem(section + 1, sections)}
    replica_after = {"dp": lax.rem(replica + 1, replicas)}
    replica_before = {"dp": lax.rem(replica + replicas - 1, replicas)}

    def remote(src, dst, s_sem, r_sem, to):
        return pltpu.make_async_remote_copy(
            src_ref=src,
            dst_ref=dst,
            send_sem=s_sem,
            recv_sem=r_sem,
            device_id=to,
            device_id_type=MESH,
        )

    load_up = pltpu.make_async_copy(up_hbm.at[0], up_w, w_sem.at[0])
    load_down = pltpu.make_async_copy(down_hbm.at[0], down_w, w_sem.at[1])
    load_up.start()
    load_down.start()

    barrier = pltpu.get_barrier_semaphore()
    partners = [chip_at(d) for d in range(1, n)]
    partners += [sibling, section_before, section_after, replica_after, replica_before]
    for partner in partners:
        pl.semaphore_signal(barrier, inc=1, device_id=partner, device_id_type=MESH)

    def stacked(ref, *at):
        left = ref[(*at, slice(None), slice(0, half))]
        right = ref[(*at, slice(None), slice(half, 2 * half))]
        return jnp.concatenate([left.astype(f32), right.astype(f32)], axis=0)

    gain_row = gain[...].astype(f32)
    gain_two = jnp.concatenate(
        [
            jnp.broadcast_to(gain_row[:, :half], (tokens, half)),
            jnp.broadcast_to(gain_row[:, half:], (tokens, half)),
        ],
        axis=0,
    )

    def feature_mean(values):
        sums = jnp.sum(values, axis=1, keepdims=True)
        both = (sums[:tokens] + sums[tokens:]) * (1.0 / (2 * half))
        return jnp.concatenate([both, both], axis=0)

    def routing(step):
        eye = lax.broadcasted_iota(jnp.int32, (rows, rows), 0) == lax.broadcasted_iota(
            jnp.int32, (rows, rows), 1
        )

        def as_row(column):
            both = jnp.concatenate([column, column], axis=0)
            return jnp.sum(jnp.where(eye, both, 0.0), axis=0, keepdims=True)

        id_rows = [as_row(ids[step, 0, :, j : j + 1].astype(f32)) for j in range(2)]
        gate_rows = [as_row(gates[step, 0, :, j : j + 1]) for j in range(2)]
        expert = lax.rem(lax.broadcasted_iota(jnp.int32, (n, rows), 0) + chip, n).astype(f32)
        named = [id_rows[j] == expert for j in range(2)]
        member = jnp.where(named[0] | named[1], 1.0, 0.0)
        gate = jnp.where(named[0], gate_rows[0], 0.0) + jnp.where(named[1], gate_rows[1], 0.0)
        r0 = lax.broadcasted_iota(jnp.int32, (rows, rows), 0)
        r1 = lax.broadcasted_iota(jnp.int32, (rows, rows), 1)
        before = (r0 < tokens) & (r0 < lax.rem(r1, tokens))
        slot = dot(member.astype(bf16), jnp.where(before, 1.0, 0.0).astype(bf16), 1, 0)
        at = lax.broadcasted_iota(jnp.int32, (block, rows), 0)
        lane = lax.broadcasted_iota(jnp.int32, (block, rows), 1)
        same_half = (at >= cap) == (lane >= tokens)
        at_slot = jnp.where(at >= cap, at - cap, at).astype(f32)
        for d in range(n):
            hit = same_half & (member[d : d + 1] > 0.5) & (slot[d : d + 1] == at_slot)
            select[step, d * block : (d + 1) * block, :] = jnp.where(hit, 1.0, 0.0).astype(bf16)
            gate_of[step, d * block : (d + 1) * block, :] = jnp.sum(
                jnp.where(hit, gate[d : d + 1], 0.0), axis=1, keepdims=True
            )

    def normed_frames(step):
        inputs = stacked(saved, step, 0)
        scale = lax.rsqrt(feature_mean(inputs * inputs) + norm_eps)
        scales[step] = scale
        return (inputs * scale * gain_two).astype(bf16)

    def fill(which, step, values, gated):
        for d in range(n):
            at = slice(d * block, (d + 1) * block)
            picked = dot(select[step, at, :], values, 1, 0)
            if gated:
                picked = picked * gate_of[step, at, :]
            target = own.at[which, 0] if d == 0 else snd.at[which, d]
            target[...] = picked.astype(bf16)

    def dispatch(which, d):
        return remote(
            snd.at[which, d],
            own.at[which, d],
            disp_s.at[which, d],
            disp_r.at[which, d],
            chip_at(d),
        )

    def forward(which, d):
        return remote(
            own.at[which, d], sib.at[which, d], fwd_s.at[which, d], fwd_r.at[which, d], sibling
        )

    order = []
    for k in range(1, n // 2):
        order += [n // 2 - k, n // 2 + k]
    order = [n // 2] + order

    def send_all(which):
        for d in order:
            dispatch(which, d).start()

    near_first = [0]
    for k in range(1, n // 2):
        near_first += [k, n - k]
    near_first += [n // 2]
    groups = [near_first[g * group : (g + 1) * group] for g in range(4)]

    def receive(which, g):
        for d in groups[g]:
            if d != 0:
                dispatch(which, d).wait_recv()
            forward(which, d).start()

    def unpack(which, g, target, first_row):
        for side, source in enumerate((own, sib)):
            if side == 1:
                for d in groups[g]:
                    forward(which, d).wait_recv()
            pieces = [source[which, d].astype(f32) for d in groups[g]]
            at = first_row + side * group * cap
            left = jnp.concatenate([p[:cap] for p in pieces], axis=0)
            right = jnp.concatenate([p[cap:] for p in pieces], axis=0)
            target[at : at + group * cap, 0:half] = left.astype(bf16)
            target[at : at + group * cap, half : 2 * half] = right.astype(bf16)

    def normed_phase(step):
        which = 2 * step
        receive(which, 0)
        for g in range(4):
            if g < 3:
                receive(which, g + 1)
            first = step * per_step + g * group_rows
            unpack(which, g, x_all, first)
            at = slice(first, first + group_rows)
            pre = dot(x_all[at, :], up_w[...], 1, 1)
            sigma = jax.nn.sigmoid(pre)
            act_all[at, :] = (pre * sigma).astype(bf16)
            slope[g * group_rows : (g + 1) * group_rows, :] = sigma * (1.0 + pre * (1.0 - sigma))

    def part_copy(step, g):
        return remote(
            part_snd.at[step, g],
            part_rcv.at[step, g],
            part_s.at[step, g],
            part_r.at[step, g],
            sibling,
        )

    def returning(step, d):
        return remote(
            ret_snd.at[step, d],
            ret_rcv.at[step, d],
            ret_s.at[step, d],
            ret_r.at[step, d],
            chip_at(n - d),
        )

    def finish_part(step, g):
        part_copy(step, g).wait_recv()
        total = part_own[g] + part_rcv[step, g].astype(f32)
        for k, d in enumerate(groups[g]):
            piece = total[k * cap : (k + 1) * cap]
            packed = jnp.concatenate([piece[:, :half], piece[:, half:]], axis=0).astype(bf16)
            if d == 0:
                ret_rcv[step, 0] = packed
            else:
                ret_snd[step, d] = packed
                returning(step, d).start()

    def grads_phase(step):
        which = 2 * step + 1
        receive(which, 0)
        for g in range(4):
            if g < 3:
                receive(which, g + 1)
            first = step * per_step + g * group_rows
            unpack(which, g, g_all, first)
            at = slice(first, first + group_rows)
            back = dot(g_all[at, :], down_w[...], 1, 1)
            hidden = (back * slope[g * group_rows : (g + 1) * group_rows, :]).astype(bf16)
            hid_all[at, :] = hidden
            part = dot(hidden, up_w[...], 1, 0)
            part_own[g] = part[: group * cap]
            part_snd[step, g] = part[group * cap :].astype(bf16)
            part_copy(step, g).start()
            if g > 0:
                finish_part(step, g - 1)

    def finish_step(step, incoming):
        for d in range(1, n):
            returning(step, d).wait_recv()
        back = ret_rcv[step].reshape(n * block, half)
        weighted = gain_two * dot(select[step], back, 0, 0)
        inputs = stacked(saved, step, 0)
        scale = scales[step]
        result = incoming + scale * weighted
        result = result - inputs * (scale * scale * scale) * feature_mean(inputs * weighted)
        result = result.astype(bf16)
        out_grads[step, 0, :, 0:half] = result[:tokens]
        out_grads[step, 0, :, half : 2 * half] = result[tokens:]
        return result

    routing(0)
    fill(0, 0, normed_frames(0), False)
    pl.semaphore_wait(barrier, len(partners))
    send_all(0)
    frames[0, 0] = stacked(in_flight, 0).astype(bf16)
    fill(1, 0, frames[0, 0], True)
    send_all(1)
    routing(1)
    fill(2, 1, normed_frames(1), False)

    load_up.wait()
    normed_phase(0)
    load_down.wait()
    grads_phase(0)
    finish_part(0, 3)

    result = finish_step(0, frames[0, 0].astype(f32))
    send_all(2)
    relay_snd[...] = result
    relay = remote(relay_snd, relay_rcv, relay_s, relay_r, section_before)
    relay.start()
    relay.wait_recv()
    last = section == sections - 1
    frames[0, 1] = jnp.where(
        last, stacked(fresh, 0), relay_rcv[...].astype(f32)
    ).astype(bf16)
    fill(3, 1, frames[0, 1], True)
    send_all(3)
    normed_phase(1)
    grads_phase(1)

    def slice_of(left, right, k):
        owner = lax.rem(replica + k, replicas)
        columns = pl.ds(pl.multiple_of(owner * quarter, quarter), quarter)
        return dot(left[...], right[:, columns], 0, 0)

    def reduce_copy(i, to):
        return remote(rs_snd.at[i], rs_rcv.at[i], rs_s.at[i], rs_r.at[i], to)

    copies = [
        reduce_copy(0, replica_before),
        reduce_copy(1, replica_after),
        reduce_copy(2, replica_after),
        reduce_copy(3, replica_before),
        reduce_copy(4, replica_after),
        reduce_copy(5, replica_before),
    ]

    def down_slice(k):
        return slice_of(act_all, g_all, k)

    def up_slice(k):
        return slice_of(hid_all, x_all, k)

    def put(i, value):
        rs_snd[i] = value.astype(bf16)
        copies[i].start()

    put(0, down_slice(2))
    put(1, down_slice(1))
    finish_part(1, 3)
    put(2, up_slice(2))
    put(3, up_slice(3))
    down_near = down_slice(3)
    copies[0].wait_recv()
    put(5, down_near + rs_rcv[0].astype(f32))
    up_near = up_slice(1)
    copies[2].wait_recv()
    put(4, up_near + rs_rcv[2].astype(f32))

    finish_step(1, frames[0, 1].astype(f32))

    down_mine = down_slice(0)
    copies[1].wait_recv()
    copies[5].wait_recv()
    out_down[0] = (down_mine + rs_rcv[1].astype(f32) + rs_rcv[5].astype(f32)).astype(bf16)
    up_mine = up_slice(0)
    copies[3].wait_recv()
    copies[4].wait_recv()
    out_up[0] = (up_mine + rs_rcv[3].astype(f32) + rs_rcv[4].astype(f32)).astype(bf16)

    for which in range(4):
        for d in range(n):
            if d != 0:
                dispatch(which, d).wait_send()
            forward(which, d).wait_send()
    for step in range(2):
        for g in range(4):
            part_copy(step, g).wait_send()
        for d in range(1, n):
            returning(step, d).wait_send()
    relay.wait_send()
    for copy in copies:
        copy.wait_send()


def local(
    mesh_sizes,
    in_flight,
    fresh_grads,
    saved_inputs,
    norm_gain,
    expert_ids,
    gate_weights,
    up_weights,
    down_weights,
):
    sections, places, replicas = mesh_sizes
    chips = places // 2
    tokens, width = saved_inputs.shape[2:]
    hidden = up_weights.shape[1]
    cap = min(tokens, 3 * tokens // chips)
    half = width // 2
    block = 2 * cap
    per_step = chips * block
    group_slots = per_step // 8
    quarter = width // replicas
    vmem = pl.BlockSpec(memory_space=pltpu.VMEM)
    anywhere = pl.BlockSpec(memory_space=pl.ANY)
    dma = pltpu.SemaphoreType.DMA
    scratch = [
        pltpu.VMEM((hidden, width), bf16),
        pltpu.VMEM((hidden, width), bf16),
        pltpu.VMEM((2, chips * block, 2 * tokens), bf16),
        pltpu.VMEM((2, chips * block, 1), f32),
        pltpu.VMEM((1, 2, 2 * tokens, half), bf16),
        pltpu.VMEM((2, 2 * tokens, 1), f32),
        pltpu.VMEM((4, chips, block, half), bf16),
        pltpu.VMEM((4, chips, block, half), bf16),
        pltpu.VMEM((4, chips, block, half), bf16),
        pltpu.VMEM((2 * per_step, width), bf16),
        pltpu.VMEM((2 * per_step, width), bf16),
        pltpu.VMEM((2 * per_step, hidden), bf16),
        pltpu.VMEM((2 * per_step, hidden), bf16),
        pltpu.VMEM((per_step, hidden), f32),
        pltpu.VMEM((4, group_slots, width), f32),
        pltpu.VMEM((2, 4, group_slots, width), bf16),
        pltpu.VMEM((2, 4, group_slots, width), bf16),
        pltpu.VMEM((2, chips, block, half), bf16),
        pltpu.VMEM((2, chips, block, half), bf16),
        pltpu.VMEM((2 * tokens, half), bf16),
        pltpu.VMEM((2 * tokens, half), bf16),
        pltpu.VMEM((6, hidden, quarter), bf16),
        pltpu.VMEM((6, hidden, quarter), bf16),
        dma((2,)),
        dma((4, chips)),
        dma((4, chips)),
        dma((4, chips)),
        dma((4, chips)),
        dma((2, 4)),
        dma((2, 4)),
        dma((2, chips)),
        dma((2, chips)),
        dma,
        dma,
        dma((6,)),
        dma((6,)),
    ]
    return tuple(
        pl.pallas_call(
            functools.partial(kernel, chips, replicas, sections, cap),
            out_shape=[
                jax.ShapeDtypeStruct((2, 1, tokens, width), bf16),
                jax.ShapeDtypeStruct((1, hidden, quarter), bf16),
                jax.ShapeDtypeStruct((1, hidden, quarter), bf16),
            ],
            in_specs=[vmem] * 6 + [anywhere] * 2,
            out_specs=[vmem] * 3,
            scratch_shapes=scratch,
            compiler_params=pltpu.CompilerParams(
                collective_id=0, has_side_effects=True, vmem_limit_bytes=56 * 2**20
            ),
        )(
            in_flight,
            fresh_grads,
            saved_inputs,
            norm_gain,
            expert_ids,
            gate_weights,
            up_weights,
            down_weights,
        )
    )


def solution(mesh):
    in_specs = (
        P("pipe", ("expert", "dp"), None),
        P(None, ("expert", "dp"), None),
        P(None, "pipe", ("expert", "dp"), None),
        P("pipe", None),
        P(None, "pipe", ("expert", "dp"), None),
        P(None, "pipe", ("expert", "dp"), None),
        P("pipe", "expert", None),
        P("pipe", "expert", None),
    )
    out_specs = (
        P(None, "pipe", ("expert", "dp"), None),
        P("pipe", "expert", "dp"),
        P("pipe", "expert", "dp"),
    )
    sizes = tuple(mesh.shape[name] for name in ("pipe", "expert", "dp"))
    return jax.shard_map(
        functools.partial(local, sizes),
        mesh=mesh,
        in_specs=in_specs,
        out_specs=out_specs,
        check_vma=False,
    )
```

time: 348 us -> 181 us (0.52)
  waiting for transfers between devices: 220 us -> 0 us
  Pallas kernels: 0 us -> 172 us
  matrix products: 44.1 us -> 0 us
  starting transfers between devices: 35.2 us -> 0 us
  between operations: 14.4 us -> 0.65 us
  other arithmetic: 13.5 us -> 0 us
  local copies, waits for them, and re-layouts: 20.2 us -> 7.24 us
    all_to_all x6 -> x0, waiting for transfers between devices: 179 us -> none  [the longest x2 67.8 us: local(): lax.all_to_all(send_grads, 'expert', split_axis=0, concat_axis=0, tiled=T...]
    pallas_call x0 -> x1, Pallas kernels: none -> 172 us  [local(): pl.pallas_call(functools.partial(kernel, chips, replicas, sections, cap),...]
    dot_general x16 -> x0, matrix products: 44.1 us -> none  [the longest x6 18.5 us: contract_rows(): lax.dot_general(left, right, (((0,), (0,)), ((), ())), preferred_element_...]
    all_to_all x6 -> x0, starting transfers between devices: 33.7 us -> none  [the longest x2 16.4 us: local(): lax.all_to_all(send_inputs, 'expert', split_axis=0, concat_axis=0, tiled=...]
    reduce_scatter x2 -> x0, waiting for transfers between devices: 33.2 us -> none  [the longest x1 33.2 us: local(): lax.psum_scatter(up_total.astype(jnp.bfloat16), 'dp', scatter_dimension=1...]
    mul x6 -> x0, local copies, waits for them, and re-layouts: 9.86 us -> none  [local(): gates[:, :, None] * incoming.astype(jnp.float32)[:, None, :]]
    ppermute x1 -> x0, waiting for transfers between devices: 7.8 us -> none  [passed_along(): return lax.ppermute(shard, axis, pairs)]
    unnamed x56 -> x7, local copies, waits for them, and re-layouts: 1.78 us -> 7.24 us
  transfers between devices with their start and end apart: 9 -> 0, of which waited for: 8 -> 0; matrix products, arithmetic and copies ran while one was open for 15% -> 0% of each run, Pallas kernels for 0% -> 0%
where the time goes in v1:
time: 181 us; the launch traced here: 180 us
  Pallas kernels  172 us (95%)
  local copies, waits for them, and re-layouts  7.24 us (4%)
    pallas_call x1, Pallas kernels, local(): pl.pallas_call(functools.partial(kernel, chips, replicas, sections, cap),...  172 us
    unnamed x7, local copies, waits for them, and re-layouts  7.24 us

profile of v1, /device:TPU:1, one launch (start us, length us, event | category | flops | bytes accessed | tf_op | source)
XLA Modules:
  0.0 180.3 jit_solution(8583261834117061074)
XLA Ops:
  0.6 1.4 copy.11.ids
  2.0 1.4 copy.12.gates
  3.5 172.4 %shard_map.103 = (bf16[2,1,64,2048]{3,2,1,0:T(8,128)(2,1)}, bf16[1,352,512]{2,1,0:T(8,128)(2,1)}, bf16[1,352,512]{2,1,0:T(8,128)(2,1)}) custom-call(bf16[1,64,2048]{2,1,0:T(8,128)(2,1)} %in_flight.1, bf16[1,64,2048]{2,1,0:T(8,128)(2,1)} %fresh.1, bf16[2,1,64,2048]{3,2,1,0:T(8,128)(2,1)} %saved.1, bf16[1,2048]{1,0:T(2,128)(2,1)} %gain.1, ...), custom_call_target="tpu_custom_call" | custom-call | tf_op jit(solution)/shard_map/pallas_call | solution.py:465
  175.9 0.0 copy-start
  175.9 1.9 %copy.16 = bf16[2,1,64,2048]{3,2,1,0:T(8,128)(2,1)} copy(bf16[2,1,64,2048]{3,2,1,0:T(8,128)(2,1)} %get-tuple-element.6) | data formatting | bytes 1048576
  177.8 1.7 copy.17
  179.6 0.0 copy-done
  179.6 0.7 copy.18
Async XLA Ops:
  175.9 3.7 %copy-start = (bf16[1,352,512]{2,1,0:T(8,128)(2,1)S(1)}, bf16[1,352,512]{2,1,0:T(8,128)(2,1)}, u32[]{:S(2)}) copy-start(bf16[1,352,512]{2,1,0:T(8,128)(2,1)} %get-tuple-element.8) | copy-start | bytes 1081348

commit v2 on v1

--- a/solution.py
+++ b/solution.py
@@ -44,11 +44,15 @@
     snd,
     own,
     sib,
+    snd_g,
+    own_g,
+    sib_g,
     x_all,
     g_all,
     act_all,
     hid_all,
     slope,
+    back_sum,
     part_own,
     part_snd,
     part_rcv,
@@ -56,8 +60,11 @@
     ret_rcv,
     relay_snd,
     relay_rcv,
-    rs_snd,
-    rs_rcv,
+    far_snd,
+    far_rcv,
+    near_snd,
+    near_rcv,
+    kept,
     w_sem,
     disp_s,
     disp_r,
@@ -69,16 +76,16 @@
     ret_r,
     relay_s,
     relay_r,
-    rs_s,
-    rs_r,
+    far_s,
+    far_r,
+    near_s,
+    near_r,
 ):
     n, cap = chips, capacity
     block = 2 * cap
     rows, half = frames.shape[2], frames.shape[3]
     tokens = rows // 2
     per_step = n * block
-    group = n // 4
-    group_rows = 2 * group * cap
     quarter = out_up.shape[2]
     place = lax.axis_index("expert")
     chip, core = place // 2, lax.rem(place, 2)
@@ -135,17 +142,12 @@
         return jnp.concatenate([both, both], axis=0)
 
     def routing(step):
-        eye = lax.broadcasted_iota(jnp.int32, (rows, rows), 0) == lax.broadcasted_iota(
-            jnp.int32, (rows, rows), 1
-        )
-
-        def as_row(column):
-            both = jnp.concatenate([column, column], axis=0)
-            return jnp.sum(jnp.where(eye, both, 0.0), axis=0, keepdims=True)
-
-        id_rows = [as_row(ids[step, 0, :, j : j + 1].astype(f32)) for j in range(2)]
-        gate_rows = [as_row(gates[step, 0, :, j : j + 1]) for j in range(2)]
-        expert = lax.rem(lax.broadcasted_iota(jnp.int32, (n, rows), 0) + chip, n).astype(f32)
+        def as_row(row):
+            return jnp.concatenate([row, row], axis=1)
+
+        id_rows = [as_row(ids[step, 0, j : j + 1, :]) for j in range(2)]
+        gate_rows = [as_row(gates[step, 0, j : j + 1, :]) for j in range(2)]
+        expert = lax.rem(lax.broadcasted_iota(jnp.int32, (n, rows), 0) + chip, n)
         named = [id_rows[j] == expert for j in range(2)]
         member = jnp.where(named[0] | named[1], 1.0, 0.0)
         gate = jnp.where(named[0], gate_rows[0], 0.0) + jnp.where(named[1], gate_rows[1], 0.0)
@@ -170,43 +172,38 @@
         scales[step] = scale
         return (inputs * scale * gain_two).astype(bf16)
 
+    def held(which, *buffers):
+        return [b.at[which] if which < 3 else g.at[which - 3] for b, g in buffers]
+
     def fill(which, step, values, gated):
+        mine, sent = held(which, (own, own_g), (snd, snd_g))
         for d in range(n):
             at = slice(d * block, (d + 1) * block)
             picked = dot(select[step, at, :], values, 1, 0)
             if gated:
                 picked = picked * gate_of[step, at, :]
-            target = own.at[which, 0] if d == 0 else snd.at[which, d]
+            target = mine.at[0] if d == 0 else sent.at[d]
             target[...] = picked.astype(bf16)
 
     def dispatch(which, d):
+        sent, mine = held(which, (snd, snd_g), (own, own_g))
         return remote(
-            snd.at[which, d],
-            own.at[which, d],
-            disp_s.at[which, d],
-            disp_r.at[which, d],
-            chip_at(d),
+            sent.at[d], mine.at[d], disp_s.at[which, d], disp_r.at[which, d], chip_at(d)
         )
 
     def forward(which, d):
-        return remote(
-            own.at[which, d], sib.at[which, d], fwd_s.at[which, d], fwd_r.at[which, d], sibling
-        )
-
-    order = []
-    for k in range(1, n // 2):
-        order += [n // 2 - k, n // 2 + k]
-    order = [n // 2] + order
-
-    def send_all(which):
-        for d in order:
-            dispatch(which, d).start()
-
-    near_first = [0]
-    for k in range(1, n // 2):
-        near_first += [k, n - k]
-    near_first += [n // 2]
-    groups = [near_first[g * group : (g + 1) * group] for g in range(4)]
+        mine, other = held(which, (own, own_g), (sib, sib_g))
+        return remote(mine.at[d], other.at[d], fwd_s.at[which, d], fwd_r.at[which, d], sibling)
+
+    groups = [[0, n // 2]] + [[k, n - k] for k in range(n // 2 - 1, 0, -1)]
+    last_group = len(groups) - 1
+    group_rows = 4 * cap
+
+    def send(which, *among):
+        for g in among:
+            for d in groups[g]:
+                if d != 0:
+                    dispatch(which, d).start()
 
     def receive(which, g):
         for d in groups[g]:
@@ -214,31 +211,28 @@
                 dispatch(which, d).wait_recv()
             forward(which, d).start()
 
-    def unpack(which, g, target, first_row):
-        for side, source in enumerate((own, sib)):
+    def unpack(which, g, target, first_row, first_column):
+        for side, source in enumerate(held(which, (own, own_g), (sib, sib_g))):
             if side == 1:
                 for d in groups[g]:
                     forward(which, d).wait_recv()
-            pieces = [source[which, d].astype(f32) for d in groups[g]]
-            at = first_row + side * group * cap
+            wide = source.shape[-1]
+            pieces = [source[d].astype(f32) for d in groups[g]]
+            at = first_row + side * 2 * cap
             left = jnp.concatenate([p[:cap] for p in pieces], axis=0)
             right = jnp.concatenate([p[cap:] for p in pieces], axis=0)
-            target[at : at + group * cap, 0:half] = left.astype(bf16)
-            target[at : at + group * cap, half : 2 * half] = right.astype(bf16)
-
-    def normed_phase(step):
-        which = 2 * step
-        receive(which, 0)
-        for g in range(4):
-            if g < 3:
-                receive(which, g + 1)
-            first = step * per_step + g * group_rows
-            unpack(which, g, x_all, first)
-            at = slice(first, first + group_rows)
-            pre = dot(x_all[at, :], up_w[...], 1, 1)
-            sigma = jax.nn.sigmoid(pre)
-            act_all[at, :] = (pre * sigma).astype(bf16)
-            slope[g * group_rows : (g + 1) * group_rows, :] = sigma * (1.0 + pre * (1.0 - sigma))
+            at = slice(at, at + 2 * cap)
+            target[at, first_column : first_column + wide] = left.astype(bf16)
+            target[at, first_column + wide : first_column + 2 * wide] = right.astype(bf16)
+
+    def take_normed(step, g):
+        first = step * per_step + g * group_rows
+        unpack(2 * step, g, x_all, first, 0)
+        at = slice(first, first + group_rows)
+        pre = dot(x_all[at, :], up_w[...], 1, 1)
+        sigma = jax.nn.sigmoid(pre)
+        act_all[at, :] = (pre * sigma).astype(bf16)
+        slope[g * group_rows : (g + 1) * group_rows, :] = sigma * (1.0 + pre * (1.0 - sigma))
 
     def part_copy(step, g):
         return remote(
@@ -270,24 +264,33 @@
                 ret_snd[step, d] = packed
                 returning(step, d).start()
 
-    def grads_phase(step):
-        which = 2 * step + 1
-        receive(which, 0)
-        for g in range(4):
-            if g < 3:
-                receive(which, g + 1)
-            first = step * per_step + g * group_rows
-            unpack(which, g, g_all, first)
-            at = slice(first, first + group_rows)
+    turns = (2, 1, 3, 0)
+
+    def columns_of(k):
+        owner = lax.rem(replica + k, replicas)
+        return pl.ds(pl.multiple_of(owner * quarter, quarter), quarter)
+
+    def hidden_back(at, j):
+        return dot(
+            g_all[at, j * quarter : (j + 1) * quarter], down_w[:, columns_of(turns[j])], 1, 1
+        )
+
+    def take_grads(step, g):
+        first = step * per_step + g * group_rows
+        at = slice(first, first + group_rows)
+        mine = slice(g * group_rows, (g + 1) * group_rows)
+        if step == 0:
+            unpack(1, g, g_all, first, 0)
             back = dot(g_all[at, :], down_w[...], 1, 1)
-            hidden = (back * slope[g * group_rows : (g + 1) * group_rows, :]).astype(bf16)
-            hid_all[at, :] = hidden
-            part = dot(hidden, up_w[...], 1, 0)
-            part_own[g] = part[: group * cap]
-            part_snd[step, g] = part[group * cap :].astype(bf16)
-            part_copy(step, g).start()
-            if g > 0:
-                finish_part(step, g - 1)
+        else:
+            unpack(4, g, g_all, first, half)
+            back = back_sum[mine, :] + hidden_back(at, 2) + hidden_back(at, 3)
+        hidden = (back * slope[mine, :]).astype(bf16)
+        hid_all[at, :] = hidden
+        part = dot(hidden, up_w[...], 1, 0)
+        part_own[g] = part[: 2 * cap]
+        part_snd[step, g] = part[2 * cap :].astype(bf16)
+        part_copy(step, g).start()
 
     def finish_step(step, incoming):
         for d in range(1, n):
@@ -306,85 +309,145 @@
     routing(0)
     fill(0, 0, normed_frames(0), False)
     pl.semaphore_wait(barrier, len(partners))
-    send_all(0)
+    send(0, 0, 1)
     frames[0, 0] = stacked(in_flight, 0).astype(bf16)
     fill(1, 0, frames[0, 0], True)
-    send_all(1)
+    send(1, 0, 1)
+    send(0, 2)
+    send(1, 2)
     routing(1)
     fill(2, 1, normed_frames(1), False)
 
     load_up.wait()
-    normed_phase(0)
     load_down.wait()
-    grads_phase(0)
-    finish_part(0, 3)
+    for g in range(last_group + 1):
+        receive(0, g)
+        receive(1, g)
+        if g + 3 <= last_group:
+            send(0, g + 3)
+            send(1, g + 3)
+        if g > 0:
+            finish_part(0, g - 1)
+        take_normed(0, g)
+        take_grads(0, g)
+    finish_part(0, last_group)
+    send(2, 0, 1)
 
     result = finish_step(0, frames[0, 0].astype(f32))
-    send_all(2)
     relay_snd[...] = result
     relay = remote(relay_snd, relay_rcv, relay_s, relay_r, section_before)
     relay.start()
+    send(2, 2, 3)
+    receive(2, 0)
+    take_normed(1, 0)
     relay.wait_recv()
     last = section == sections - 1
-    frames[0, 1] = jnp.where(
-        last, stacked(fresh, 0), relay_rcv[...].astype(f32)
-    ).astype(bf16)
-    fill(3, 1, frames[0, 1], True)
-    send_all(3)
-    normed_phase(1)
-    grads_phase(1)
-
-    def slice_of(left, right, k):
+    frames[0, 1] = jnp.where(last, stacked(fresh, 0), relay_rcv[...].astype(f32)).astype(bf16)
+
+    def quarter_of(k):
         owner = lax.rem(replica + k, replicas)
-        columns = pl.ds(pl.multiple_of(owner * quarter, quarter), quarter)
-        return dot(left[...], right[:, columns], 0, 0)
-
-    def reduce_copy(i, to):
-        return remote(rs_snd.at[i], rs_rcv.at[i], rs_s.at[i], rs_r.at[i], to)
-
-    copies = [
-        reduce_copy(0, replica_before),
-        reduce_copy(1, replica_after),
-        reduce_copy(2, replica_after),
-        reduce_copy(3, replica_before),
-        reduce_copy(4, replica_after),
-        reduce_copy(5, replica_before),
-    ]
-
-    def down_slice(k):
-        return slice_of(act_all, g_all, k)
-
-    def up_slice(k):
-        return slice_of(hid_all, x_all, k)
-
-    def put(i, value):
-        rs_snd[i] = value.astype(bf16)
-        copies[i].start()
-
-    put(0, down_slice(2))
-    put(1, down_slice(1))
-    finish_part(1, 3)
-    put(2, up_slice(2))
-    put(3, up_slice(3))
-    down_near = down_slice(3)
-    copies[0].wait_recv()
-    put(5, down_near + rs_rcv[0].astype(f32))
-    up_near = up_slice(1)
-    copies[2].wait_recv()
-    put(4, up_near + rs_rcv[2].astype(f32))
-
+        side = pl.multiple_of((owner // 2) * tokens, tokens)
+        within = pl.multiple_of(lax.rem(owner, 2) * quarter, quarter)
+        return frames[0, 1, pl.ds(side, tokens), pl.ds(within, quarter)]
+
+    for j in range(2):
+        pair = [quarter_of(turns[2 * j]), quarter_of(turns[2 * j + 1])]
+        fill(3 + j, 1, jnp.concatenate(pair, axis=0), True)
+        if j == 0:
+            send(3, 0, 1, 2, 3)
+    for g in range(1, last_group + 1):
+        receive(2, g)
+        take_normed(1, g)
+    send(4, 0, 1, 2, 3)
+
+    hidden_half = far_snd.shape[2]
+    halves = [slice(0, hidden_half), slice(hidden_half, 2 * hidden_half)]
+    ways = [replica_after, replica_before]
+    down, up = 0, 1
+
+    def slice_of(kind, k):
+        if kind == up:
+            return dot(hid_all[...], x_all[:, columns_of(k)], 0, 0)
+        j = turns.index(k)
+        first = dot(act_all[:per_step, :], g_all[:per_step, columns_of(k)], 0, 0)
+        return first + dot(
+            act_all[per_step:, :], g_all[per_step:, j * quarter : (j + 1) * quarter], 0, 0
+        )
+
+    def far(kind, way):
+        return remote(
+            far_snd.at[kind, way],
+            far_rcv.at[kind, way],
+            far_s.at[kind, way],
+            far_r.at[kind, way],
+            ways[way],
+        )
+
+    def close(kind, way, part):
+        return remote(
+            near_snd.at[kind, way, part],
+            near_rcv.at[kind, way, part],
+            near_s.at[kind, way, part],
+            near_r.at[kind, way, part],
+            ways[way],
+        )
+
+    def send_far(kind):
+        value = slice_of(kind, 2)
+        for way in range(2):
+            far_snd[kind, way] = value[halves[way]].astype(bf16)
+            far(kind, way).start()
+
+    def send_near(kind, way):
+        value = slice_of(kind, (1, 3)[way])
+        near_snd[kind, way, 1 - way] = value[halves[1 - way]].astype(bf16)
+        close(kind, way, 1 - way).start()
+        kept[kind, way] = value[halves[way]]
+
+    def merge(kind, way):
+        far(kind, way).wait_recv()
+        near_snd[kind, way, way] = (kept[kind, way] + far_rcv[kind, way].astype(f32)).astype(bf16)
+        close(kind, way, way).start()
+
+    def finish_sum(kind, out):
+        value = slice_of(kind, 0)
+        for part in range(2):
+            total = value[halves[part]]
+            for way in range(2):
+                close(kind, way, part).wait_recv()
+                total = total + near_rcv[kind, way, part].astype(f32)
+            out[0, halves[part], :] = total.astype(bf16)
+
+    for g in range(last_group + 1):
+        receive(3, g)
+        if g > 0:
+            unpack(3, g - 1, g_all, per_step + (g - 1) * group_rows, 0)
+    unpack(3, last_group, g_all, per_step + last_group * group_rows, 0)
+    send_far(down)
+    send_near(down, 0)
+    at = slice(per_step, 2 * per_step)
+    back_sum[...] = hidden_back(at, 0) + hidden_back(at, 1)
+    receive(4, 0)
+    for g in range(last_group + 1):
+        if g < last_group:
+            receive(4, g + 1)
+        take_grads(1, g)
+        if g > 0:
+            finish_part(1, g - 1)
+    send_near(down, 1)
+    merge(down, 0)
+    send_far(up)
+    finish_part(1, last_group)
+    merge(down, 1)
+    send_near(up, 0)
+    send_near(up, 1)
+    merge(up, 0)
+    merge(up, 1)
     finish_step(1, frames[0, 1].astype(f32))
-
-    down_mine = down_slice(0)
-    copies[1].wait_recv()
-    copies[5].wait_recv()
-    out_down[0] = (down_mine + rs_rcv[1].astype(f32) + rs_rcv[5].astype(f32)).astype(bf16)
-    up_mine = up_slice(0)
-    copies[3].wait_recv()
-    copies[4].wait_recv()
-    out_up[0] = (up_mine + rs_rcv[3].astype(f32) + rs_rcv[4].astype(f32)).astype(bf16)
-
-    for which in range(4):
+    finish_sum(down, out_down)
+    finish_sum(up, out_up)
+
+    for which in range(5):
         for d in range(n):
             if d != 0:
                 dispatch(which, d).wait_send()
@@ -395,8 +458,11 @@
         for d in range(1, n):
             returning(step, d).wait_send()
     relay.wait_send()
-    for copy in copies:
-        copy.wait_send()
+    for kind in range(2):
+        for way in range(2):
+            far(kind, way).wait_send()
+            for part in range(2):
+                close(kind, way, part).wait_send()
 
 
 def local(
@@ -430,13 +496,17 @@
         pltpu.VMEM((2, chips * block, 1), f32),
         pltpu.VMEM((1, 2, 2 * tokens, half), bf16),
         pltpu.VMEM((2, 2 * tokens, 1), f32),
-        pltpu.VMEM((4, chips, block, half), bf16),
-        pltpu.VMEM((4, chips, block, half), bf16),
-        pltpu.VMEM((4, chips, block, half), bf16),
+        pltpu.VMEM((3, chips, block, half), bf16),
+        pltpu.VMEM((3, chips, block, half), bf16),
+        pltpu.VMEM((3, chips, block, half), bf16),
+        pltpu.VMEM((2, chips, block, quarter), bf16),
+        pltpu.VMEM((2, chips, block, quarter), bf16),
+        pltpu.VMEM((2, chips, block, quarter), bf16),
         pltpu.VMEM((2 * per_step, width), bf16),
         pltpu.VMEM((2 * per_step, width), bf16),
         pltpu.VMEM((2 * per_step, hidden), bf16),
         pltpu.VMEM((2 * per_step, hidden), bf16),
+        pltpu.VMEM((per_step, hidden), f32),
         pltpu.VMEM((per_step, hidden), f32),
         pltpu.VMEM((4, group_slots, width), f32),
         pltpu.VMEM((2, 4, group_slots, width), bf16),
@@ -445,29 +515,34 @@
         pltpu.VMEM((2, chips, block, half), bf16),
         pltpu.VMEM((2 * tokens, half), bf16),
         pltpu.VMEM((2 * tokens, half), bf16),
-        pltpu.VMEM((6, hidden, quarter), bf16),
-        pltpu.VMEM((6, hidden, quarter), bf16),
+        pltpu.VMEM((2, 2, hidden // 2, quarter), bf16),
+        pltpu.VMEM((2, 2, hidden // 2, quarter), bf16),
+        pltpu.VMEM((2, 2, 2, hidden // 2, quarter), bf16),
+        pltpu.VMEM((2, 2, 2, hidden // 2, quarter), bf16),
+        pltpu.VMEM((2, 2, hidden // 2, quarter), f32),
         dma((2,)),
-        dma((4, chips)),
-        dma((4, chips)),
-        dma((4, chips)),
-        dma((4, chips)),
+        dma((5, chips)),
+        dma((5, chips)),
+        dma((5, chips)),
+        dma((5, chips)),
         dma((2, 4)),
         dma((2, 4)),
         dma((2, chips)),
         dma((2, chips)),
         dma,
         dma,
-        dma((6,)),
-        dma((6,)),
+        dma((2, 2)),
+        dma((2, 2)),
+        dma((2, 2, 2)),
+        dma((2, 2, 2)),
     ]
     return tuple(
         pl.pallas_call(
             functools.partial(kernel, chips, replicas, sections, cap),
             out_shape=[
-                jax.ShapeDtypeStruct((2, 1, tokens, width), bf16),
-                jax.ShapeDtypeStruct((1, hidden, quarter), bf16),
-                jax.ShapeDtypeStruct((1, hidden, quarter), bf16),
+                pltpu.VMEM((2, 1, tokens, width), bf16),
+                pltpu.VMEM((1, hidden, quarter), bf16),
+                pltpu.VMEM((1, hidden, quarter), bf16),
             ],
             in_specs=[vmem] * 6 + [anywhere] * 2,
             out_specs=[vmem] * 3,
@@ -480,8 +555,8 @@
             fresh_grads,
             saved_inputs,
             norm_gain,
-            expert_ids,
-            gate_weights,
+            jnp.swapaxes(expert_ids, 2, 3),
+            jnp.swapaxes(gate_weights, 2, 3),
             up_weights,
             down_weights,
         )

time: 181 us -> 151 us (0.83)
  the two profiles are of different devices: /device:TPU:1 before, /device:TPU:15 now
where the time goes in v2:
time: 151 us
  Pallas kernels  148 us (98%)
  local copies, waits for them, and re-layouts  2.27 us (2%)
    pallas_call x1, Pallas kernels, local(): pl.pallas_call(functools.partial(kernel, chips, replicas, sections, cap),...  148 us

profile of v2, /device:TPU:15, one launch (start us, length us, event | category | flops | bytes accessed | tf_op | source)
XLA Modules:
  0.0 151.3 jit_solution(15516249556127106656)
XLA Ops:
  0.6 148.4 %shard_map.103 = (bf16[2,1,64,2048]{3,2,1,0:T(8,128)(2,1)S(1)}, bf16[1,352,512]{2,1,0:T(8,128)(2,1)S(1)}, bf16[1,352,512]{2,1,0:T(8,128)(2,1)S(1)}) custom-call(bf16[1,64,2048]{2,1,0:T(8,128)(2,1)} %in_flight.1, bf16[1,64,2048]{2,1,0:T(8,128)(2,1)} %fresh.1, bf16[2,1,64,2048]{3,2,1,0:T(8,128)(2,1)} %saved.1, bf16[1,2048]{1,0:T(2,128)(2,1)} %gain.1, ...), custom_call_target="tpu_custom_call" | custom-call | tf_op jit(solution)/shard_map/pallas_call | solution.py:540
  149.0 0.8 copy.14
  149.8 0.7 copy.15
  150.6 0.7 copy.16

commit v3 on v2

--- a/solution.py
+++ b/solution.py
@@ -24,9 +24,9 @@
     replicas,
     sections,
     capacity,
-    in_flight,
-    fresh,
-    saved,
+    in_flight_hbm,
+    fresh_hbm,
+    saved_hbm,
     gain,
     ids,
     gates,
@@ -37,6 +37,9 @@
     out_down,
     up_w,
     down_w,
+    in_flight,
+    fresh,
+    saved,
     select,
     gate_of,
     frames,
@@ -52,7 +55,12 @@
     act_all,
     hid_all,
     slope,
-    back_sum,
+    info_snd,
+    info_rcv,
+    cols_snd,
+    cols_rcv,
+    act_oth,
+    g_oth,
     part_own,
     part_snd,
     part_rcv,
@@ -80,6 +88,12 @@
     far_r,
     near_s,
     near_r,
+    info_s,
+    info_r,
+    cols_s,
+    cols_r,
+    act_s,
+    act_r,
 ):
     n, cap = chips, capacity
     block = 2 * cap
@@ -100,6 +114,11 @@
     section_after = {"pipe": lax.rem(section + 1, sections)}
     replica_after = {"dp": lax.rem(replica + 1, replicas)}
     replica_before = {"dp": lax.rem(replica + replicas - 1, replicas)}
+    others = (2, 1, 3)
+
+    def replica_at(k):
+        return {"dp": lax.rem(replica + k, replicas)}
+
 
     def remote(src, dst, s_sem, r_sem, to):
         return pltpu.make_async_remote_copy(
@@ -111,16 +130,24 @@
             device_id_type=MESH,
         )
 
-    load_up = pltpu.make_async_copy(up_hbm.at[0], up_w, w_sem.at[0])
-    load_down = pltpu.make_async_copy(down_hbm.at[0], down_w, w_sem.at[1])
-    load_up.start()
-    load_down.start()
-
     barrier = pltpu.get_barrier_semaphore()
     partners = [chip_at(d) for d in range(1, n)]
-    partners += [sibling, section_before, section_after, replica_after, replica_before]
+    partners += [sibling, section_before, section_after]
+    partners += [replica_at(k) for k in others]
     for partner in partners:
         pl.semaphore_signal(barrier, inc=1, device_id=partner, device_id_type=MESH)
+
+    moves = [
+        (saved_hbm.at[0, 0], saved.at[0]),
+        (in_flight_hbm.at[0], in_flight),
+        (saved_hbm.at[1, 0], saved.at[1]),
+        (up_hbm.at[0], up_w),
+        (down_hbm.at[0], down_w),
+        (fresh_hbm.at[0], fresh),
+    ]
+    loads = [pltpu.make_async_copy(a, b, w_sem.at[i]) for i, (a, b) in enumerate(moves)]
+    for load in loads:
+        load.start()
 
     def stacked(ref, *at):
         left = ref[(*at, slice(None), slice(0, half))]
@@ -141,13 +168,18 @@
         both = (sums[:tokens] + sums[tokens:]) * (1.0 / (2 * half))
         return jnp.concatenate([both, both], axis=0)
 
-    def routing(step):
-        def as_row(row):
-            return jnp.concatenate([row, row], axis=1)
-
-        id_rows = [as_row(ids[step, 0, j : j + 1, :]) for j in range(2)]
-        gate_rows = [as_row(gates[step, 0, j : j + 1, :]) for j in range(2)]
-        expert = lax.rem(lax.broadcasted_iota(jnp.int32, (n, rows), 0) + chip, n)
+    def as_rows(step):
+        both = [
+            ids[step, 0].astype(f32),
+            gates[step, 0],
+        ]
+        four = jnp.concatenate(both, axis=0)
+        return jnp.concatenate([four, four], axis=1)
+
+    def routing(step, table):
+        id_rows = [table[j : j + 1] for j in range(2)]
+        gate_rows = [table[2 + j : 3 + j] for j in range(2)]
+        expert = lax.rem(lax.broadcasted_iota(jnp.int32, (n, rows), 0) + chip, n).astype(f32)
         named = [id_rows[j] == expert for j in range(2)]
         member = jnp.where(named[0] | named[1], 1.0, 0.0)
         gate = jnp.where(named[0], gate_rows[0], 0.0) + jnp.where(named[1], gate_rows[1], 0.0)
@@ -167,17 +199,17 @@
             )
 
     def normed_frames(step):
-        inputs = stacked(saved, step, 0)
+        inputs = stacked(saved, step)
         scale = lax.rsqrt(feature_mean(inputs * inputs) + norm_eps)
         scales[step] = scale
-        return (inputs * scale * gain_two).astype(bf16)
+        frames[1, step] = (inputs * scale * gain_two).astype(bf16)
 
     def held(which, *buffers):
-        return [b.at[which] if which < 3 else g.at[which - 3] for b, g in buffers]
-
-    def fill(which, step, values, gated):
+        return [b.at[which] if which < 4 else g.at[which - 4] for b, g in buffers]
+
+    def fill(which, step, values, gated, *among):
         mine, sent = held(which, (own, own_g), (snd, snd_g))
-        for d in range(n):
+        for d in [d for g in among for d in groups[g]]:
             at = slice(d * block, (d + 1) * block)
             picked = dot(select[step, at, :], values, 1, 0)
             if gated:
@@ -264,27 +296,16 @@
                 ret_snd[step, d] = packed
                 returning(step, d).start()
 
-    turns = (2, 1, 3, 0)
-
     def columns_of(k):
         owner = lax.rem(replica + k, replicas)
         return pl.ds(pl.multiple_of(owner * quarter, quarter), quarter)
-
-    def hidden_back(at, j):
-        return dot(
-            g_all[at, j * quarter : (j + 1) * quarter], down_w[:, columns_of(turns[j])], 1, 1
-        )
 
     def take_grads(step, g):
         first = step * per_step + g * group_rows
         at = slice(first, first + group_rows)
         mine = slice(g * group_rows, (g + 1) * group_rows)
-        if step == 0:
-            unpack(1, g, g_all, first, 0)
-            back = dot(g_all[at, :], down_w[...], 1, 1)
-        else:
-            unpack(4, g, g_all, first, half)
-            back = back_sum[mine, :] + hidden_back(at, 2) + hidden_back(at, 3)
+        unpack(2 * step + 1, g, g_all, first, 0)
+        back = dot(g_all[at, :], down_w[...], 1, 1)
         hidden = (back * slope[mine, :]).astype(bf16)
         hid_all[at, :] = hidden
         part = dot(hidden, up_w[...], 1, 0)
@@ -297,7 +318,7 @@
             returning(step, d).wait_recv()
         back = ret_rcv[step].reshape(n * block, half)
         weighted = gain_two * dot(select[step], back, 0, 0)
-        inputs = stacked(saved, step, 0)
+        inputs = stacked(saved, step)
         scale = scales[step]
         result = incoming + scale * weighted
         result = result - inputs * (scale * scale * scale) * feature_mean(inputs * weighted)
@@ -306,20 +327,127 @@
         out_grads[step, 0, :, half : 2 * half] = result[tokens:]
         return result
 
-    routing(0)
-    fill(0, 0, normed_frames(0), False)
+    hidden_half = far_snd.shape[2]
+    halves = [slice(0, hidden_half), slice(hidden_half, 2 * hidden_half)]
+    ways = [replica_after, replica_before]
+    down, up = 0, 1
+
+    def slice_of(kind, k):
+        if kind == up:
+            return dot(hid_all[...], x_all[:, columns_of(k)], 0, 0)
+        return dot(act_all[:per_step, :], g_all[:per_step, columns_of(k)], 0, 0)
+
+    def far(kind, way):
+        return remote(
+            far_snd.at[kind, way],
+            far_rcv.at[kind, way],
+            far_s.at[kind, way],
+            far_r.at[kind, way],
+            ways[way],
+        )
+
+    def close(kind, way, part):
+        return remote(
+            near_snd.at[kind, way, part],
+            near_rcv.at[kind, way, part],
+            near_s.at[kind, way, part],
+            near_r.at[kind, way, part],
+            ways[way],
+        )
+
+    def send_far(kind):
+        value = slice_of(kind, 2)
+        for way in range(2):
+            far_snd[kind, way] = value[halves[way]].astype(bf16)
+            far(kind, way).start()
+
+    def send_near(kind, way):
+        value = slice_of(kind, (1, 3)[way])
+        near_snd[kind, way, 1 - way] = value[halves[1 - way]].astype(bf16)
+        close(kind, way, 1 - way).start()
+        kept[kind, way] = value[halves[way]]
+
+    def merge(kind, way):
+        far(kind, way).wait_recv()
+        near_snd[kind, way, way] = (kept[kind, way] + far_rcv[kind, way].astype(f32)).astype(bf16)
+        close(kind, way, way).start()
+
+    def info_copy(k):
+        return remote(info_snd, info_rcv.at[k - 1], info_s.at[k - 1], info_r.at[k - 1], replica_at(k))
+
+    def cols_copy(k):
+        return remote(
+            cols_snd.at[k - 1],
+            cols_rcv.at[k - 1],
+            cols_s.at[k - 1],
+            cols_r.at[k - 1],
+            replica_at(k),
+        )
+
+    def act_copy(way):
+        return remote(
+            act_all.at[pl.ds(per_step, per_step)],
+            act_oth.at[2 * way],
+            act_s.at[way],
+            act_r.at[way],
+            ways[way],
+        )
+
+    def act_onward(way):
+        part = pl.ds(way * (per_step // 2), per_step // 2)
+        return remote(
+            act_oth.at[2 * way, part],
+            act_oth.at[1, part],
+            act_s.at[2 + way],
+            act_r.at[2 + way],
+            ways[way],
+        )
+
+    def later_down():
+        value = dot(act_all[per_step:, :], g_all[per_step:, columns_of(0)], 0, 0)
+        for way in range(2):
+            act_onward(way).wait_recv()
+        for k in others:
+            first = (k - 1) * per_step
+            value = value + dot(act_oth[k - 1], g_oth[first : first + per_step, :], 0, 0)
+        return value
+
+    def finish_sum(kind, out):
+        value = slice_of(kind, 0)
+        if kind == down:
+            value = value + later_down()
+        for part in range(2):
+            total = value[halves[part]]
+            for way in range(2):
+                close(kind, way, part).wait_recv()
+                total = total + near_rcv[kind, way, part].astype(f32)
+            out[0, halves[part], :] = total.astype(bf16)
+
+    every = range(last_group + 1)
+    routing(0, as_rows(0))
+    loads[0].wait()
+    normed_frames(0)
+    fill(0, 0, frames[1, 0], False, 0, 1)
     pl.semaphore_wait(barrier, len(partners))
     send(0, 0, 1)
-    frames[0, 0] = stacked(in_flight, 0).astype(bf16)
-    fill(1, 0, frames[0, 0], True)
+    loads[1].wait()
+    frames[0, 0] = stacked(in_flight).astype(bf16)
+    fill(1, 0, frames[0, 0], True, 0, 1)
     send(1, 0, 1)
+    fill(0, 0, frames[1, 0], False, 2, 3)
+    fill(1, 0, frames[0, 0], True, 2, 3)
     send(0, 2)
     send(1, 2)
-    routing(1)
-    fill(2, 1, normed_frames(1), False)
-
-    load_up.wait()
-    load_down.wait()
+    info_snd[...] = as_rows(1)
+    for k in others:
+        info_copy(k).start()
+    routing(1, info_snd[...])
+    loads[2].wait()
+    normed_frames(1)
+    fill(2, 1, frames[1, 1], False, *every)
+
+    loads[3].wait()
+    loads[4].wait()
     for g in range(last_group + 1):
         receive(0, g)
         receive(1, g)
@@ -332,17 +460,26 @@
         take_grads(0, g)
     finish_part(0, last_group)
     send(2, 0, 1)
+    send_far(down)
+    send_near(down, 0)
+    send_near(down, 1)
+    for k in others:
+        info_copy(k).wait_recv()
+        routing(1 + k, info_rcv[k - 1])
 
     result = finish_step(0, frames[0, 0].astype(f32))
     relay_snd[...] = result
     relay = remote(relay_snd, relay_rcv, relay_s, relay_r, section_before)
     relay.start()
     send(2, 2, 3)
+    for way in range(2):
+        merge(down, way)
     receive(2, 0)
     take_normed(1, 0)
     relay.wait_recv()
     last = section == sections - 1
-    frames[0, 1] = jnp.where(last, stacked(fresh, 0), relay_rcv[...].astype(f32)).astype(bf16)
+    loads[5].wait()
+    frames[0, 1] = jnp.where(last, stacked(fresh), relay_rcv[...].astype(f32)).astype(bf16)
 
     def quarter_of(k):
         owner = lax.rem(replica + k, replicas)
@@ -350,104 +487,54 @@
         within = pl.multiple_of(lax.rem(owner, 2) * quarter, quarter)
         return frames[0, 1, pl.ds(side, tokens), pl.ds(within, quarter)]
 
-    for j in range(2):
-        pair = [quarter_of(turns[2 * j]), quarter_of(turns[2 * j + 1])]
-        fill(3 + j, 1, jnp.concatenate(pair, axis=0), True)
-        if j == 0:
-            send(3, 0, 1, 2, 3)
-    for g in range(1, last_group + 1):
+    fill(3, 1, frames[0, 1], True, *every)
+    send(3, 0, 1)
+    for k in others:
+        whole = quarter_of(k)
+        pair = [whole[:, : quarter // 2], whole[:, quarter // 2 :]]
+        cols_snd[k - 1] = jnp.concatenate(pair, axis=0)
+        cols_copy(k).start()
+    for g in every[1:]:
         receive(2, g)
         take_normed(1, g)
-    send(4, 0, 1, 2, 3)
-
-    hidden_half = far_snd.shape[2]
-    halves = [slice(0, hidden_half), slice(hidden_half, 2 * hidden_half)]
-    ways = [replica_after, replica_before]
-    down, up = 0, 1
-
-    def slice_of(kind, k):
-        if kind == up:
-            return dot(hid_all[...], x_all[:, columns_of(k)], 0, 0)
-        j = turns.index(k)
-        first = dot(act_all[:per_step, :], g_all[:per_step, columns_of(k)], 0, 0)
-        return first + dot(
-            act_all[per_step:, :], g_all[per_step:, j * quarter : (j + 1) * quarter], 0, 0
-        )
-
-    def far(kind, way):
-        return remote(
-            far_snd.at[kind, way],
-            far_rcv.at[kind, way],
-            far_s.at[kind, way],
-            far_r.at[kind, way],
-            ways[way],
-        )
-
-    def close(kind, way, part):
-        return remote(
-            near_snd.at[kind, way, part],
-            near_rcv.at[kind, way, part],
-            near_s.at[kind, way, part],
-            near_r.at[kind, way, part],
-            ways[way],
-        )
-
-    def send_far(kind):
-        value = slice_of(kind, 2)
-        for way in range(2):
-            far_snd[kind, way] = value[halves[way]].astype(bf16)
-            far(kind, way).start()
-
-    def send_near(kind, way):
-        value = slice_of(kind, (1, 3)[way])
-        near_snd[kind, way, 1 - way] = value[halves[1 - way]].astype(bf16)
-        close(kind, way, 1 - way).start()
-        kept[kind, way] = value[halves[way]]
-
-    def merge(kind, way):
-        far(kind, way).wait_recv()
-        near_snd[kind, way, way] = (kept[kind, way] + far_rcv[kind, way].astype(f32)).astype(bf16)
-        close(kind, way, way).start()
-
-    def finish_sum(kind, out):
-        value = slice_of(kind, 0)
-        for part in range(2):
-            total = value[halves[part]]
-            for way in range(2):
-                close(kind, way, part).wait_recv()
-                total = total + near_rcv[kind, way, part].astype(f32)
-            out[0, halves[part], :] = total.astype(bf16)
-
-    for g in range(last_group + 1):
-        receive(3, g)
-        if g > 0:
-            unpack(3, g - 1, g_all, per_step + (g - 1) * group_rows, 0)
-    unpack(3, last_group, g_all, per_step + last_group * group_rows, 0)
-    send_far(down)
-    send_near(down, 0)
-    at = slice(per_step, 2 * per_step)
-    back_sum[...] = hidden_back(at, 0) + hidden_back(at, 1)
-    receive(4, 0)
-    for g in range(last_group + 1):
+        if g == 2:
+            send(3, 2)
+    send(3, 3)
+    for way in range(2):
+        act_copy(way).start()
+    receive(3, 0)
+    for g in every:
         if g < last_group:
-            receive(4, g + 1)
+            receive(3, g + 1)
         take_grads(1, g)
+        if g == last_group - 1:
+            for k in others:
+                cols_copy(k).wait_recv()
+                fill(3 + k, 1 + k, cols_rcv[k - 1], True, *every)
+                send(3 + k, *every)
         if g > 0:
             finish_part(1, g - 1)
-    send_near(down, 1)
-    merge(down, 0)
+        if g == last_group - 1:
+            for way in range(2):
+                act_copy(way).wait_recv()
+                act_onward(way).start()
     send_far(up)
     finish_part(1, last_group)
-    merge(down, 1)
     send_near(up, 0)
     send_near(up, 1)
     merge(up, 0)
     merge(up, 1)
+    for k in others:
+        for g in every:
+            receive(3 + k, g)
     finish_step(1, frames[0, 1].astype(f32))
+    for k in others:
+        for g in every:
+            unpack(3 + k, g, g_oth, (k - 1) * per_step + g * group_rows, 0)
     finish_sum(down, out_down)
     finish_sum(up, out_up)
 
-    for which in range(5):
+    for which in range(7):
         for d in range(n):
             if d != 0:
                 dispatch(which, d).wait_send()
@@ -458,6 +545,12 @@
         for d in range(1, n):
             returning(step, d).wait_send()
     relay.wait_send()
+    for k in others:
+        info_copy(k).wait_send()
+        cols_copy(k).wait_send()
+    for way in range(2):
+        act_copy(way).wait_send()
+        act_onward(way).wait_send()
     for kind in range(2):
         for way in range(2):
             far(kind, way).wait_send()
@@ -492,22 +585,30 @@
     scratch = [
         pltpu.VMEM((hidden, width), bf16),
         pltpu.VMEM((hidden, width), bf16),
-        pltpu.VMEM((2, chips * block, 2 * tokens), bf16),
-        pltpu.VMEM((2, chips * block, 1), f32),
-        pltpu.VMEM((1, 2, 2 * tokens, half), bf16),
+        pltpu.VMEM((tokens, width), bf16),
+        pltpu.VMEM((tokens, width), bf16),
+        pltpu.VMEM((2, tokens, width), bf16),
+        pltpu.VMEM((5, chips * block, 2 * tokens), bf16),
+        pltpu.VMEM((5, chips * block, 1), f32),
+        pltpu.VMEM((2, 2, 2 * tokens, half), bf16),
         pltpu.VMEM((2, 2 * tokens, 1), f32),
-        pltpu.VMEM((3, chips, block, half), bf16),
-        pltpu.VMEM((3, chips, block, half), bf16),
-        pltpu.VMEM((3, chips, block, half), bf16),
-        pltpu.VMEM((2, chips, block, quarter), bf16),
-        pltpu.VMEM((2, chips, block, quarter), bf16),
-        pltpu.VMEM((2, chips, block, quarter), bf16),
+        pltpu.VMEM((4, chips, block, half), bf16),
+        pltpu.VMEM((4, chips, block, half), bf16),
+        pltpu.VMEM((4, chips, block, half), bf16),
+        pltpu.VMEM((3, chips, block, quarter // 2), bf16),
+        pltpu.VMEM((3, chips, block, quarter // 2), bf16),
+        pltpu.VMEM((3, chips, block, quarter // 2), bf16),
         pltpu.VMEM((2 * per_step, width), bf16),
         pltpu.VMEM((2 * per_step, width), bf16),
         pltpu.VMEM((2 * per_step, hidden), bf16),
         pltpu.VMEM((2 * per_step, hidden), bf16),
         pltpu.VMEM((per_step, hidden), f32),
-        pltpu.VMEM((per_step, hidden), f32),
+        pltpu.VMEM((4, 2 * tokens), f32),
+        pltpu.VMEM((3, 4, 2 * tokens), f32),
+        pltpu.VMEM((3, 2 * tokens, quarter // 2), bf16),
+        pltpu.VMEM((3, 2 * tokens, quarter // 2), bf16),
+        pltpu.VMEM((3, per_step, hidden), bf16),
+        pltpu.VMEM((3 * per_step, quarter), bf16),
         pltpu.VMEM((4, group_slots, width), f32),
         pltpu.VMEM((2, 4, group_slots, width), bf16),
         pltpu.VMEM((2, 4, group_slots, width), bf16),
@@ -520,11 +621,11 @@
         pltpu.VMEM((2, 2, 2, hidden // 2, quarter), bf16),
         pltpu.VMEM((2, 2, 2, hidden // 2, quarter), bf16),
         pltpu.VMEM((2, 2, hidden // 2, quarter), f32),
-        dma((2,)),
-        dma((5, chips)),
-        dma((5, chips)),
-        dma((5, chips)),
-        dma((5, chips)),
+        dma((6,)),
+        dma((7, chips)),
+        dma((7, chips)),
+        dma((7, chips)),
+        dma((7, chips)),
         dma((2, 4)),
         dma((2, 4)),
         dma((2, chips)),
@@ -535,6 +636,12 @@
         dma((2, 2)),
         dma((2, 2, 2)),
         dma((2, 2, 2)),
+        dma((3,)),
+        dma((3,)),
+        dma((3,)),
+        dma((3,)),
+        dma((4,)),
+        dma((4,)),
     ]
     return tuple(
         pl.pallas_call(
@@ -544,7 +651,7 @@
                 pltpu.VMEM((1, hidden, quarter), bf16),
                 pltpu.VMEM((1, hidden, quarter), bf16),
             ],
-            in_specs=[vmem] * 6 + [anywhere] * 2,
+            in_specs=[anywhere] * 3 + [vmem] * 3 + [anywhere] * 2,
             out_specs=[vmem] * 3,
             scratch_shapes=scratch,
             compiler_params=pltpu.CompilerParams(

time: 151 us -> 145 us (0.960)
  the two profiles are of different devices: /device:TPU:15 before, /device:TPU:1 now
where the time goes in v3:
time: 145 us
  Pallas kernels  142 us (98%)
  local copies, waits for them, and re-layouts  2.27 us (2%)
    pallas_call x1, Pallas kernels, local(): pl.pallas_call(functools.partial(kernel, chips, replicas, sections, cap),...  142 us

profile of v3, /device:TPU:1, one launch (start us, length us, event | category | flops | bytes accessed | tf_op | source)
XLA Modules:
  0.0 145.0 jit_solution(6759537660567780860)
XLA Ops:
  0.6 142.0 %shard_map.103 = (bf16[2,1,64,2048]{3,2,1,0:T(8,128)(2,1)S(1)}, bf16[1,352,512]{2,1,0:T(8,128)(2,1)S(1)}, bf16[1,352,512]{2,1,0:T(8,128)(2,1)S(1)}) custom-call(bf16[1,64,2048]{2,1,0:T(8,128)(2,1)} %in_flight_hbm.1, bf16[1,64,2048]{2,1,0:T(8,128)(2,1)} %fresh_hbm.1, bf16[2,1,64,2048]{3,2,1,0:T(8,128)(2,1)} %saved_hbm.1, bf16[1,2048]{1,0:T(2,128)(2,1)} %gain.1, ...), custom_call_target="tpu_custom_call" | custom-call | tf_op jit(solution)/shard_map/pallas_call | solution.py:647
  142.7 0.8 copy.14
  143.5 0.7 copy.15
  144.2 0.7 copy.16

commit v4 on v3

--- a/solution.py
+++ b/solution.py
@@ -470,16 +470,20 @@
     result = finish_step(0, frames[0, 0].astype(f32))
     relay_snd[...] = result
     relay = remote(relay_snd, relay_rcv, relay_s, relay_r, section_before)
-    relay.start()
+    pl.when(section > 0)(relay.start)
     send(2, 2, 3)
     for way in range(2):
         merge(down, way)
     receive(2, 0)
     take_normed(1, 0)
-    relay.wait_recv()
-    last = section == sections - 1
+    pl.when(section < sections - 1)(relay.wait_recv)
     loads[5].wait()
-    frames[0, 1] = jnp.where(last, stacked(fresh), relay_rcv[...].astype(f32)).astype(bf16)
+
+    @pl.when(section == sections - 1)
+    def _():
+        relay_rcv[...] = stacked(fresh).astype(bf16)
+
+    frames[0, 1] = relay_rcv[...]
 
     def quarter_of(k):
         owner = lax.rem(replica + k, replicas)
@@ -544,7 +548,7 @@
             part_copy(step, g).wait_send()
         for d in range(1, n):
             returning(step, d).wait_send()
-    relay.wait_send()
+    pl.when(section > 0)(relay.wait_send)
     for k in others:
         info_copy(k).wait_send()
         cols_copy(k).wait_send()

time: 145 us -> 144 us (level)
  Pallas kernels: 142 us -> 140 us
    pallas_call x1, Pallas kernels: 142 us -> 140 us  [local(): pl.pallas_call(functools.partial(kernel, chips, replicas, sections, cap),...]
where the time goes in v4:
time: 144 us; the launch traced here: 143 us
  Pallas kernels  140 us (97%)
  local copies, waits for them, and re-layouts  2.27 us (2%)
    pallas_call x1, Pallas kernels, local(): pl.pallas_call(functools.partial(kernel, chips, replicas, sections, cap),...  140 us

profile of v4, /device:TPU:1, one launch (start us, length us, event | category | flops | bytes accessed | tf_op | source)
XLA Modules:
  0.0 143.3 jit_solution(16544056800557236819)
XLA Ops:
  0.6 140.4 %shard_map.103 = (bf16[2,1,64,2048]{3,2,1,0:T(8,128)(2,1)S(1)}, bf16[1,352,512]{2,1,0:T(8,128)(2,1)S(1)}, bf16[1,352,512]{2,1,0:T(8,128)(2,1)S(1)}) custom-call(bf16[1,64,2048]{2,1,0:T(8,128)(2,1)} %in_flight_hbm.1, bf16[1,64,2048]{2,1,0:T(8,128)(2,1)} %fresh_hbm.1, bf16[2,1,64,2048]{3,2,1,0:T(8,128)(2,1)} %saved_hbm.1, bf16[1,2048]{1,0:T(2,128)(2,1)} %gain.1, ...), custom_call_target="tpu_custom_call" | custom-call | tf_op jit(solution)/shard_map/pallas_call | solution.py:651
  141.1 0.8 copy.14
  141.9 0.7 copy.15
  142.6 0.7 copy.16

commit v5 on v4

--- a/solution.py
+++ b/solution.py
@@ -27,9 +27,9 @@
     in_flight_hbm,
     fresh_hbm,
     saved_hbm,
-    gain,
-    ids,
-    gates,
+    gain_hbm,
+    ids_hbm,
+    gates_hbm,
     up_hbm,
     down_hbm,
     out_grads,
@@ -40,6 +40,9 @@
     in_flight,
     fresh,
     saved,
+    gain,
+    ids,
+    gates,
     select,
     gate_of,
     frames,
@@ -144,10 +147,15 @@
         (up_hbm.at[0], up_w),
         (down_hbm.at[0], down_w),
         (fresh_hbm.at[0], fresh),
+        (ids_hbm, ids),
+        (gates_hbm, gates),
+        (gain_hbm, gain),
     ]
     loads = [pltpu.make_async_copy(a, b, w_sem.at[i]) for i, (a, b) in enumerate(moves)]
-    for load in loads:
+    for load in loads[6:] + loads[:6]:
         load.start()
+    for load in loads[6:]:
+        load.wait()
 
     def stacked(ref, *at):
         left = ref[(*at, slice(None), slice(0, half))]
@@ -592,6 +600,9 @@
         pltpu.VMEM((tokens, width), bf16),
         pltpu.VMEM((tokens, width), bf16),
         pltpu.VMEM((2, tokens, width), bf16),
+        pltpu.VMEM((1, width), bf16),
+        pltpu.VMEM((2, 1, 2, tokens), jnp.int32),
+        pltpu.VMEM((2, 1, 2, tokens), f32),
         pltpu.VMEM((5, chips * block, 2 * tokens), bf16),
         pltpu.VMEM((5, chips * block, 1), f32),
         pltpu.VMEM((2, 2, 2 * tokens, half), bf16),
@@ -625,7 +636,7 @@
         pltpu.VMEM((2, 2, 2, hidden // 2, quarter), bf16),
         pltpu.VMEM((2, 2, 2, hidden // 2, quarter), bf16),
         pltpu.VMEM((2, 2, hidden // 2, quarter), f32),
-        dma((6,)),
+        dma((9,)),
         dma((7, chips)),
         dma((7, chips)),
         dma((7, chips)),
@@ -655,7 +666,7 @@
                 pltpu.VMEM((1, hidden, quarter), bf16),
                 pltpu.VMEM((1, hidden, quarter), bf16),
             ],
-            in_specs=[anywhere] * 3 + [vmem] * 3 + [anywhere] * 2,
+            in_specs=[anywhere] * 8,
             out_specs=[vmem] * 3,
             scratch_shapes=scratch,
             compiler_params=pltpu.CompilerParams(

time: 144 us -> 143 us (level)
  no operation moved by 1% of the time
where the time goes in v5:
time: 143 us
  Pallas kernels  140 us (98%)
  local copies, waits for them, and re-layouts  2.27 us (2%)
    pallas_call x1, Pallas kernels, local(): pl.pallas_call(functools.partial(kernel, chips, replicas, sections, cap),...  140 us

profile of v5, /device:TPU:1, one launch (start us, length us, event | category | flops | bytes accessed | tf_op | source)
XLA Modules:
  0.0 142.8 jit_solution(12514519096855422067)
XLA Ops:
  0.6 139.8 %shard_map.103 = (bf16[2,1,64,2048]{3,2,1,0:T(8,128)(2,1)S(1)}, bf16[1,352,512]{2,1,0:T(8,128)(2,1)S(1)}, bf16[1,352,512]{2,1,0:T(8,128)(2,1)S(1)}) custom-call(bf16[1,64,2048]{2,1,0:T(8,128)(2,1)} %in_flight_hbm.1, bf16[1,64,2048]{2,1,0:T(8,128)(2,1)} %fresh_hbm.1, bf16[2,1,64,2048]{3,2,1,0:T(8,128)(2,1)} %saved_hbm.1, bf16[1,2048]{1,0:T(2,128)(2,1)} %gain_hbm.1, ...), custom_call_target="tpu_custom_call" | custom-call | tf_op jit(solution)/shard_map/pallas_call | solution.py:662
  140.5 0.8 copy.14
  141.3 0.7 copy.15
  142.0 0.7 copy.16
